TPU v7x, 256 devices: a whole 4x4x8 slice. The times are simulated.
256 devices in a mesh: gx: 16 (over z, x_lo), mode: 16 (over y, x_hi, core).
Axes of the slice: x: 4 (x_hi: 2, x_lo: 2; x = x_hi * 2 + x_lo), y: 4, z: 8, core: 2. Of those that a mesh axis runs over, the one named last changes fastest.
Arguments:
- section_field: bfloat16 [1024, 2, 64, 4, 128], P('mode', None, 'gx'), may hold values from -6 to 6
- base_field: bfloat16 [1024, 2, 64, 4, 128], P('mode', None, 'gx'), may hold values from -6 to 6
- prev_rate: float32 [1024, 2, 64, 4, 128], P('mode', None, 'gx'), may hold values from -6 to 6
- block_list: int32 [16, 5], P('mode'), may hold values from 0 to 15, as said below
- coupling: bfloat16 [16, 5, 5, 64, 64], P('mode'), may hold values from -0.3125 to 0.3125
- diffusivity: float32 [2], replicated, may hold values from 0.05 to 0.25
- reaction_fields: bfloat16 [4, 64, 4, 128], P(None, 'gx'), may hold values from -2 to 2
- species_mix: float32 [2, 2], replicated, may hold values from -1 to 1
Outputs:
- rate: float32 [1024, 2, 64, 4, 128], P('mode', None, 'gx')
- next_field: bfloat16 [1024, 2, 64, 4, 128], P('mode', None, 'gx')
Inputs may be any that keep to these rules, and one draw needn't show every extreme that they name: `block_list`: row i lists block i first, then 5 - 2 other different blocks, each at a cyclic distance of 1 to 2 from i, then block (i + 8) modulo 16.
All inputs are finite; a program needn't handle non-finite values.
Results may differ from a plain program's by a relative error of at most 0.0022.
Values may be sent and summed in bfloat16 or wider, within the bound.
A program may use at most 64 MiB of HBM per device.

v0:
```python
import jax
import jax.numpy as jnp
from jax import lax
from jax.sharding import PartitionSpec as P

MB = 64
K = 4


half_step = 0.25


def padded_2(cells, sides, width):
    for axis, dim in sides:
        count = lax.axis_size(axis)
        head = lax.slice_in_dim(cells, 0, width, axis=dim)
        tail = lax.slice_in_dim(cells, cells.shape[dim] - width, cells.shape[dim], axis=dim)
        cells = jnp.concatenate(
            [
                lax.ppermute(tail, axis, [(i, (i + 1) % count) for i in range(count)]),
                cells,
                lax.ppermute(head, axis, [((i + 1) % count, i) for i in range(count)]),
            ],
            axis=dim,
        )
    return cells


def stencil(padded):
    values = padded.astype(jnp.float32)
    center = values[:, :, 1:-1]
    total = values[:, :, 2:] + values[:, :, :-2]
    total = total + jnp.roll(center, 1, 3) + jnp.roll(center, -1, 3)
    total = total + jnp.roll(center, 1, 4) + jnp.roll(center, -1, 4)
    return (total - 6.0 * center).astype(jnp.bfloat16)


def shards(
    section_field,
    base_field,
    prev_rate,
    block_list,
    coupling,
    diffusivity,
    reaction_fields,
    species_mix,
):
    rows_own, species, planes, depth, width = section_field.shape
    grid_cells = planes * depth * width
    cells = species * grid_cells
    own_blocks = rows_own // MB
    padded = padded_2(section_field, (("gx", 2),), 1)
    fields = reaction_fields.astype(jnp.float32).reshape(K, 1, grid_cells)
    fields = jnp.broadcast_to(fields, (K, species, grid_cells)).reshape(K, cells)
    start_state = (
        jnp.zeros((own_blocks, MB, cells), jnp.float32),
        jnp.zeros((own_blocks, MB, cells), jnp.float32),
    )

    def add_block(carry, fetch, index):
        hits_all = block_list == index

        def update(state):
            lap_block, field_block = fetch()
            diffusion, reaction = state
            hits = hits_all[0]
            slot = jnp.argmax(hits.astype(jnp.int32))
            chosen = lax.dynamic_index_in_dim(coupling[0], slot, 0, False)
            found = jnp.any(hits).astype(jnp.float32)
            diff_term = jnp.dot(chosen[0], lap_block, preferred_element_type=jnp.float32)
            react_term = fields[0] * jnp.dot(
                chosen[1], field_block, preferred_element_type=jnp.float32
            )
            for term in range(1, K):
                react_term = react_term + fields[term] * jnp.dot(
                    chosen[1 + term], field_block, preferred_element_type=jnp.float32
                )
            diffusion = diffusion.at[0].add(found * diff_term)
            reaction = reaction.at[0].add(found * react_term)
            return (diffusion, reaction)

        def unchanged(state):
            return state

        return lax.cond(jnp.any(hits_all), update, unchanged, carry)

    def lap_fetcher(lap_piece, field_piece, offset):

        def fetch():
            lap_block = lax.dynamic_slice_in_dim(lap_piece, offset, MB, 0).reshape(MB, cells)
            field_block = lax.dynamic_slice_in_dim(field_piece, offset, MB, 0).reshape(MB, cells)
            return (lap_block, field_block)

        return fetch

    own_lap = stencil(padded)
    lap_piece = lax.all_gather(own_lap, "mode", axis=0, tiled=True)
    field_piece = lax.all_gather(section_field, "mode", axis=0, tiled=True)
    count = lap_piece.shape[0] // MB

    def each_block(number, state):
        fetch = lap_fetcher(lap_piece, field_piece, number * MB)
        return add_block(state, fetch, number)

    diffusion, reaction = lax.fori_loop(0, count, each_block, start_state)
    diffusion = diffusion.reshape(rows_own, species, planes, depth, width)
    reaction = reaction.reshape(rows_own, species, planes, depth, width)
    current = section_field.astype(jnp.float32)
    mixed_parts = []
    for target in range(species):
        total = species_mix[target, 0] * current[:, 0]
        total = total + species_mix[target, 1] * current[:, 1]
        mixed_parts.append(total)
    mixing = jnp.stack(mixed_parts, axis=1)
    rate = diffusivity[None, :, None, None, None] * diffusion - reaction + mixing
    next_field = (base_field.astype(jnp.float32) + half_step * (prev_rate + rate)).astype(
        jnp.bfloat16
    )
    return (rate, next_field)


def solution(mesh):
    placed = (
        P("mode", None, "gx", None, None),
        P("mode", None, "gx", None, None),
        P("mode", None, "gx", None, None),
        P("mode", None),
        P("mode", None, None, None, None),
        P(),
        P(None, "gx", None, None),
        P(),
    )
    return jax.shard_map(
        shards,
        mesh=mesh,
        in_specs=placed,
        out_specs=(P("mode", None, "gx", None, None), P("mode", None, "gx", None, None)),
        check_vma=False,
    )
```

profile of v0, /device:TPU:5, one launch (start us, length us, event | category | flops | bytes accessed | tf_op | source)
XLA Modules:
  0.0 284.6 jit_solution(6950745412351231852)
XLA Ops:
  10.0 5.4 %collective-permute-start.1 = (bf16[64,2,1,4,128]{4,3,2,1,0:T(4,128)(2,1)S(1)}, bf16[64,2,1,4,128]{4,3,2,1,0:T(4,128)(2,1)S(1)}, u32[]{:S(2)}, u32[]{:S(2)}) collective-permute-start(bf16[64,2,1,4,128]{4,3,2,1,0:T(4,128)(2,1)S(1)} %get-tuple-element.281), channel_id=1, source_target_pairs={{16,0},{32,16},{48,32},{64,48},{80,64},{96,80},{112,96},{128,112},... | collective-permute-start | bytes 393224 | tf_op jit(solution)/shard_map/ppermute | solution.py:22
  15.4 3.1 %collective-permute-done = bf16[64,2,1,4,128]{4,3,2,1,0:T(4,128)(2,1)S(1)} collective-permute-done((bf16[64,2,1,4,128]{4,3,2,1,0:T(4,128)(2,1)S(1)}, bf16[64,2,1,4,128]{4,3,2,1,0:T(4,128)(2,1)S(1)}, u32[]{:S(2)}, u32[]{:S(2)}) %collective-permute-start) | collective-permute-done | bytes 131104 | tf_op jit(solution)/shard_map/ppermute | solution.py:20
  18.5 1.6 maximum_convert_fusion
  22.4 2.9 %fusion.16 = bf16[64,2,4,4,128]{4,3,2,1,0:T(4,128)(2,1)} fusion(f32[64,2,6,4,128]{4,3,2,1,0:T(4,128)S(1)} %maximum_convert_fusion, f32[64,2,4,3,128]{4,3,2,1,0:T(4,128)S(1)} %get-tuple-element.275, f32[64,2,4,1,128]{4,3,2,1,0:T(1,128)S(1)} %get-tuple-element.277, f32[64,2,4,1,128]{4,3,2,1,0:T(1,128)S(1)} %get-tuple-element.276, ...), kind=kLoop, calls=%fused_computation.31 | loop fusion | flops 3145728 | bytes 7864320 | tf_op jit(solution)/shard_map/convert_element_type | solution.py:35
  26.7 3.6 %multiply_add_fusion.1 = (f32[64,1,4,4,128]{4,3,2,1,0:T(4,128)}, f32[64,1,4,4,128]{4,3,2,1,0:T(4,128)}) fusion(f32[64,2,4,4,128]{4,3,2,1,0:T(4,128)S(1)} %convert_element_type.36, f32[]{:T(128)} %bitcast.13, f32[]{:T(128)} %bitcast.12, f32[]{:T(128)} %bitcast.15, f32[]{:T(128)} %bitcast.14), kind=kLoop, calls=%fused_computation.41 | loop fusion | flops 786432 | bytes 2097168 | tf_op jit(solution)/shard_map/add | solution.py:112
  30.4 59.4 %all-gather.5.cloned.1.call-done = bf16[1024,2,4,4,128]{4,3,2,1,0:T(4,128)(2,1)} async-done(((bf16[64,2,4,4,128]{4,3,2,1,0:T(4,128)(2,1)}), bf16[1024,2,4,4,128]{4,3,2,1,0:T(4,128)(2,1)}) %all-gather.5.cloned.1.call-update) | async-done | bytes 8388624 | tf_op jit(solution)/shard_map/all_gather | solution.py:98
  89.7 79.2 %all-gather.3.cloned.1.call-done = bf16[1024,2,4,4,128]{4,3,2,1,0:T(4,128)(2,1)} async-done(((bf16[64,2,4,4,128]{4,3,2,1,0:T(4,128)(2,1)}), bf16[1024,2,4,4,128]{4,3,2,1,0:T(4,128)(2,1)}) %all-gather.3.cloned.1.call-update) | async-done | bytes 8388624 | tf_op jit(solution)/shard_map/all_gather | solution.py:97
  171.1 99.1 %while.18 = (s32[]{:T(128)}, f32[1,64,4096]{2,1,0:T(8,128)}, f32[1,64,4096]{2,1,0:T(8,128)}, s32[1,5]{1,0:T(1,128)S(1)}, bf16[1,5,5,64,64]{4,3,2,1,0:T(8,128)(2,...) while((s32[]{:T(128)}, f32[1,64,4096]{2,1,0:T(8,128)}, ...), condition=%wide.region_6.7_spmd.clone, body=%wide.region_0.6_spmd.clone.sunk | while | flops 170655808 | bytes 17809840 | solution.py:105
  173.8 15.5 %conditional.3 = ((f32[1,64,4096]{2,1,0:T(8,128)}, f32[1,64,4096]{2,1,0:T(8,128)})) conditional(s32[]{:T(128)} %convert_element_type.47, (f32[1,64,4096]{2,1,0:T(8,128)}, f32[1,64,4096]{2,1,0:T(8,128)}) %tuple.76, (pred[1,5]{1,0:T(4,128)(4,1)S(1)}, bf16[1,5,5,64,64]{4,3,2,1,0:T(8,128)(2,1)}, s32[]{:T(128)}, bf16[1024,2,4,4,128]{4,3,2,1,0:T(4,128)(2,1)}, ...), branch_computations={%region_2.2_spmd, %region_3.5_spmd} | conditional | flops 170655792 | bytes 17809632 | solution.py:85
  176.2 1.6 constant_dynamic-slice_fusion
  180.3 2.0 convolution_multiply_fusion.2
  183.5 2.9 %fusion.8 = f32[1,64,4096]{2,1,0:T(8,128)} fusion(f32[1,64,4096]{2,1,0:T(8,128)} %get-tuple-element.201, f32[64,4096]{1,0:T(8,128)S(1)} %convolution_multiply_fusion, f32[64,4096]{1,0:T(8,128)S(1)} %convolution_multiply_fusion.1, f32[64,4096]{1,0:T(8,128)} %convolution_multiply_fusion.2, bf16[64,4096]{1,0:T(8,128)(2,1)S(1)} %reshape.105, ...), kind=kOutput, calls=%fused_computation.12 | convolution fusion | flops 35127296 | bytes 5799948 | tf_op jit(solution)/shard_map/while/body/eval_jaxpr/cond/branch_1_fun/dot_general | solution.py:71
  186.8 2.5 fusion.9
  192.0 15.5 %conditional.3 = ((f32[1,64,4096]{2,1,0:T(8,128)}, f32[1,64,4096]{2,1,0:T(8,128)})) conditional(s32[]{:T(128)} %convert_element_type.47, (f32[1,64,4096]{2,1,0:T(8,128)}, f32[1,64,4096]{2,1,0:T(8,128)}) %tuple.76, (pred[1,5]{1,0:T(4,128)(4,1)S(1)}, bf16[1,5,5,64,64]{4,3,2,1,0:T(8,128)(2,1)}, s32[]{:T(128)}, bf16[1024,2,4,4,128]{4,3,2,1,0:T(4,128)(2,1)}, ...), branch_computations={%region_2.2_spmd, %region_3.5_spmd} | conditional | flops 170655792 | bytes 17809632 | solution.py:85
  198.5 2.0 convolution_multiply_fusion.2
  201.7 2.9 %fusion.8 = f32[1,64,4096]{2,1,0:T(8,128)} fusion(f32[1,64,4096]{2,1,0:T(8,128)} %get-tuple-element.201, f32[64,4096]{1,0:T(8,128)S(1)} %convolution_multiply_fusion, f32[64,4096]{1,0:T(8,128)S(1)} %convolution_multiply_fusion.1, f32[64,4096]{1,0:T(8,128)} %convolution_multiply_fusion.2, bf16[64,4096]{1,0:T(8,128)(2,1)S(1)} %reshape.105, ...), kind=kOutput, calls=%fused_computation.12 | convolution fusion | flops 35127296 | bytes 5799948 | tf_op jit(solution)/shard_map/while/body/eval_jaxpr/cond/branch_1_fun/dot_general | solution.py:71
  205.0 2.5 fusion.9
  208.8 15.5 %conditional.3 = ((f32[1,64,4096]{2,1,0:T(8,128)}, f32[1,64,4096]{2,1,0:T(8,128)})) conditional(s32[]{:T(128)} %convert_element_type.47, (f32[1,64,4096]{2,1,0:T(8,128)}, f32[1,64,4096]{2,1,0:T(8,128)}) %tuple.76, (pred[1,5]{1,0:T(4,128)(4,1)S(1)}, bf16[1,5,5,64,64]{4,3,2,1,0:T(8,128)(2,1)}, s32[]{:T(128)}, bf16[1024,2,4,4,128]{4,3,2,1,0:T(4,128)(2,1)}, ...), branch_computations={%region_2.2_spmd, %region_3.5_spmd} | conditional | flops 170655792 | bytes 17809632 | solution.py:85
  215.4 2.0 convolution_multiply_fusion.2
  218.5 2.9 %fusion.8 = f32[1,64,4096]{2,1,0:T(8,128)} fusion(f32[1,64,4096]{2,1,0:T(8,128)} %get-tuple-element.201, f32[64,4096]{1,0:T(8,128)S(1)} %convolution_multiply_fusion, f32[64,4096]{1,0:T(8,128)S(1)} %convolution_multiply_fusion.1, f32[64,4096]{1,0:T(8,128)} %convolution_multiply_fusion.2, bf16[64,4096]{1,0:T(8,128)(2,1)S(1)} %reshape.105, ...), kind=kOutput, calls=%fused_computation.12 | convolution fusion | flops 35127296 | bytes 5799948 | tf_op jit(solution)/shard_map/while/body/eval_jaxpr/cond/branch_1_fun/dot_general | solution.py:71
  221.9 2.5 fusion.9
  225.7 15.5 %conditional.3 = ((f32[1,64,4096]{2,1,0:T(8,128)}, f32[1,64,4096]{2,1,0:T(8,128)})) conditional(s32[]{:T(128)} %convert_element_type.47, (f32[1,64,4096]{2,1,0:T(8,128)}, f32[1,64,4096]{2,1,0:T(8,128)}) %tuple.76, (pred[1,5]{1,0:T(4,128)(4,1)S(1)}, bf16[1,5,5,64,64]{4,3,2,1,0:T(8,128)(2,1)}, s32[]{:T(128)}, bf16[1024,2,4,4,128]{4,3,2,1,0:T(4,128)(2,1)}, ...), branch_computations={%region_2.2_spmd, %region_3.5_spmd} | conditional | flops 170655792 | bytes 17809632 | solution.py:85
  232.2 2.0 convolution_multiply_fusion.2
  235.4 2.9 %fusion.8 = f32[1,64,4096]{2,1,0:T(8,128)} fusion(f32[1,64,4096]{2,1,0:T(8,128)} %get-tuple-element.201, f32[64,4096]{1,0:T(8,128)S(1)} %convolution_multiply_fusion, f32[64,4096]{1,0:T(8,128)S(1)} %convolution_multiply_fusion.1, f32[64,4096]{1,0:T(8,128)} %convolution_multiply_fusion.2, bf16[64,4096]{1,0:T(8,128)(2,1)S(1)} %reshape.105, ...), kind=kOutput, calls=%fused_computation.12 | convolution fusion | flops 35127296 | bytes 5799948 | tf_op jit(solution)/shard_map/while/body/eval_jaxpr/cond/branch_1_fun/dot_general | solution.py:71
  238.7 2.5 fusion.9
  249.3 15.5 %conditional.3 = ((f32[1,64,4096]{2,1,0:T(8,128)}, f32[1,64,4096]{2,1,0:T(8,128)})) conditional(s32[]{:T(128)} %convert_element_type.47, (f32[1,64,4096]{2,1,0:T(8,128)}, f32[1,64,4096]{2,1,0:T(8,128)}) %tuple.76, (pred[1,5]{1,0:T(4,128)(4,1)S(1)}, bf16[1,5,5,64,64]{4,3,2,1,0:T(8,128)(2,1)}, s32[]{:T(128)}, bf16[1024,2,4,4,128]{4,3,2,1,0:T(4,128)(2,1)}, ...), branch_computations={%region_2.2_spmd, %region_3.5_spmd} | conditional | flops 170655792 | bytes 17809632 | solution.py:85
  255.8 2.0 convolution_multiply_fusion.2
  259.0 2.9 %fusion.8 = f32[1,64,4096]{2,1,0:T(8,128)} fusion(f32[1,64,4096]{2,1,0:T(8,128)} %get-tuple-element.201, f32[64,4096]{1,0:T(8,128)S(1)} %convolution_multiply_fusion, f32[64,4096]{1,0:T(8,128)S(1)} %convolution_multiply_fusion.1, f32[64,4096]{1,0:T(8,128)} %convolution_multiply_fusion.2, bf16[64,4096]{1,0:T(8,128)(2,1)S(1)} %reshape.105, ...), kind=kOutput, calls=%fused_computation.12 | convolution fusion | flops 35127296 | bytes 5799948 | tf_op jit(solution)/shard_map/while/body/eval_jaxpr/cond/branch_1_fun/dot_general | solution.py:71
  262.3 2.5 fusion.9
  270.2 1.9 reshape.111
  272.2 2.0 reshape.112
  274.3 3.5 %add_convert_fusion = (bf16[64,2,4,4,128]{4,3,2,1,0:T(4,128)(2,1)}, f32[64,2,4,4,128]{4,3,2,1,0:T(4,128)}) fusion(f32[64,2,4,4,128]{4,3,2,1,0:T(4,128)} %param.18, bf16[64,2,4,4,128]{4,3,2,1,0:T(4,128)(2,1)} %param.17, f32[64,1,4,4,128]{4,3,2,1,0:T(4,128)S(1)} %copy-done.2, f32[64,1,4,4,128]{4,3,2,1,0:T(4,128)S(1)} %copy-done.1, ...), kind=kLoop, calls=%fused_computation.38 | loop fusion | flops 2359296 | bytes 6291464 | tf_op jit(solution)/shard_map/convert_element_type | solution.py:116
  (106 shorter events, 47.2 us)
Async XLA Ops:
  7.2 82.6 %all-gather.5.cloned.1.call-start = ((), (), s32[]{:S(2)}) async-start(), calls=%async_computation.1 | async-start | bytes 8912896 | tf_op jit(solution)/shard_map/all_gather | solution.py:98
  7.9 161.1 %all-gather.3.cloned.1.call-start = ((), (), s32[]{:S(2)}) async-start(), calls=%async_computation | async-start | bytes 8912896 | tf_op jit(solution)/shard_map/all_gather | solution.py:97
  9.0 9.5 %collective-permute-start = (bf16[64,2,1,4,128]{4,3,2,1,0:T(4,128)(2,1)S(1)}, bf16[64,2,1,4,128]{4,3,2,1,0:T(4,128)(2,1)S(1)}, u32[]{:S(2)}, u32[]{:S(2)}) collective-permute-start(bf16[64,2,1,4,128]{4,3,2,1,0:T(4,128)(2,1)S(1)} %get-tuple-element.280), channel_id=1, source_target_pairs={{0,16},{16,32},{32,48},{48,64},{64,80},{80,96},{96,112},{112,128},... | collective-permute-start | bytes 393224 | tf_op jit(solution)/shard_map/ppermute | solution.py:20
  10.0 8.5 %collective-permute-start.1 = (bf16[64,2,1,4,128]{4,3,2,1,0:T(4,128)(2,1)S(1)}, bf16[64,2,1,4,128]{4,3,2,1,0:T(4,128)(2,1)S(1)}, u32[]{:S(2)}, u32[]{:S(2)}) collective-permute-start(bf16[64,2,1,4,128]{4,3,2,1,0:T(4,128)(2,1)S(1)} %get-tuple-element.281), channel_id=1, source_target_pairs={{16,0},{32,16},{48,32},{64,48},{80,64},{96,80},{112,96},{128,112},... | collective-permute-start | bytes 393224 | tf_op jit(solution)/shard_map/ppermute | solution.py:22
  22.4 3.0 %copy-start = (bf16[64,2,4,4,128]{4,3,2,1,0:T(4,128)(2,1)S(1)}, bf16[64,2,4,4,128]{4,3,2,1,0:T(4,128)(2,1)}, u32[]{:S(2)}) copy-start(bf16[64,2,4,4,128]{4,3,2,1,0:T(4,128)(2,1)} %param.16) | copy-start | bytes 1572868
  25.4 0.7 copy-start.3
  25.4 0.7 copy-start.5
  30.4 140.7 %copy-start.4 = (s32[1,5]{1,0:T(1,128)S(1)}, s32[1,5]{1,0:T(1,128)}, u32[]{:S(2)}) copy-start(s32[1,5]{1,0:T(1,128)} %param.19) | copy-start | bytes 64
  272.2 2.1 copy-start.1
  272.2 2.1 copy-start.2
  272.2 2.1 copy-start.6
Sparse Core Ops, SparseCore 0:
  10.8 78.9 all-gather.4
  93.1 75.8 all-gather.2
where the time goes:
time: 290 us; the launch traced here: 285 us
  waiting for transfers between devices  142 us (49%)
  matrix products  47.1 us (16%)
  other arithmetic  29.5 us (10%)
  local copies, waits for them, and re-layouts  22.8 us (8%)
  loops' own time  22.1 us (8%)
  between operations  14.2 us (5%)
  starting transfers between devices  6.45 us (2%)
    all_gather x1, waiting for transfers between devices, shards(): lap_piece = lax.all_gather(own_lap, 'mode', axis=0, tiled=True)  79.2 us
    all_gather x1, waiting for transfers between devices, shards(): field_piece = lax.all_gather(section_field, 'mode', axis=0, tiled=True)  59.4 us
    dot_general x15, matrix products, update(): jnp.dot(chosen[1 + term], field_block, preferred_element_type=jnp.float32)  19.9 us
    dot_general x5, matrix products, update(): jnp.dot(chosen[1], field_block, preferred_element_type=jnp.float32)  14.7 us
    dot_general x5, matrix products, update(): jnp.dot(chosen[0], lap_block, preferred_element_type=jnp.float32)  12.5 us
    another operation x16, loops' own time, add_block(): return lax.cond(jnp.any(hits_all), update, unchanged, carry)  11.8 us
    reduce_or x16, other arithmetic, add_block(): return lax.cond(jnp.any(hits_all), update, unchanged, carry)  11 us
    another operation x1, loops' own time, shards(): diffusion, reaction = lax.fori_loop(0, count, each_block, start_state)  10.3 us
  transfers between devices with their start and end apart: 4, of which 3 were waited for; matrix products, arithmetic and copies ran while one was open for 4% of the time, Pallas kernels for 0%

commit v1 on v0

v1 whole, which is shorter than its diff:
```python
import jax
import jax.numpy as jnp
from jax import lax
from jax.sharding import PartitionSpec as P
import jax.experimental.pallas as pl
import jax.experimental.pallas.tpu as pltpu

MB = 64
NBLK = 16
K = 4
TERMS = 1 + K
NNZ = 5
MESH = pl.DeviceIdType.MESH

half_step = 0.25

OWN, SIB, ACROSS, CROSS, RELAY, SIB2 = range(6)
TRANSIT, HALO_LO, HALO_HI = 6, 7, 8
PLANES = (0, 3, 1, 2)
STRIDE = 32


def kernel(
    section_hbm,
    coupling_hbm,
    fields_hbm,
    blocks_ref,
    diffusivity_ref,
    mix_ref,
    out_ref,
    native,
    wide,
    couple,
    fields_in,
    fields,
    blocks,
    transit,
    weights,
    diff,
    react,
    edge,
    halo,
    local_sem,
    send_sem,
    recv_sem,
):
    g = lax.axis_index("gx")
    i = lax.axis_index("mode")
    y = i // 4
    h = lax.rem(i // 2, 2)
    c = lax.rem(i, 2)
    step = 1 - 2 * h

    def device(dy, hh, cc):
        return (g, lax.rem(y + dy + 4, 4) * 4 + hh * 2 + cc)

    at_cross = device(0, 1 - h, c)
    at_relay = device(step, h, c)
    at_back = device(-step, h, c)
    at_across = device(2, h, c)
    at_sib = device(0, h, 1 - c)
    at_up = (lax.rem(g + 1, 16), i)
    at_down = (lax.rem(g + 15, 16), i)

    load = pltpu.make_async_copy(section_hbm, native, local_sem.at[0])
    load.start()
    load_couple = pltpu.make_async_copy(coupling_hbm, couple, local_sem.at[1])
    load_couple.start()
    load_fields = pltpu.make_async_copy(fields_hbm, fields_in, local_sem.at[2])
    load_fields.start()

    barrier = pltpu.get_barrier_semaphore()
    for peer in (at_cross, at_relay, at_back, at_across, at_sib, at_up, at_down):
        pl.semaphore_signal(barrier, inc=1, device_id=peer, device_id_type=MESH)

    load.wait()

    @pl.loop(0, 8)
    def _(n):
        rows = pl.ds(pl.multiple_of(n * 256, 256), 256)
        wide[rows, :] = native[rows, :].astype(jnp.float32)

    for pos, plane in enumerate(PLANES):

        @pl.loop(0, 8)
        def _(sy, pos=pos, plane=plane):
            start = (sy // 4) * 16 + plane * 4 + lax.rem(sy, 4)
            blocks[OWN, pos, sy] = wide[pl.ds(start, MB, stride=STRIDE), :].astype(jnp.bfloat16)

    pl.semaphore_wait(barrier, 7)

    def send(kind, part, source, target, peer):
        return pltpu.make_async_remote_copy(
            src_ref=source,
            dst_ref=target,
            send_sem=send_sem.at[kind, part],
            recv_sem=recv_sem.at[kind, part],
            device_id=peer,
            device_id_type=MESH,
        )

    def part_of(slot, part):
        return blocks.at[slot, pl.ds(2 * part, 2)]

    def block_send(source, target, part, peer):
        return send(target, part, part_of(source, part), part_of(target, part), peer)

    cross = [block_send(OWN, CROSS, p, at_cross) for p in (0, 1)]
    relay = [block_send(CROSS, RELAY, p, at_relay) for p in (0, 1)]
    transit_send = send(TRANSIT, 1, part_of(OWN, 1), transit, at_back)
    across = [
        block_send(OWN, ACROSS, 0, at_across),
        send(ACROSS, 1, transit, part_of(ACROSS, 1), at_back),
    ]
    sib = send(SIB, 0, blocks.at[OWN], blocks.at[SIB], at_sib)
    sib_cross = [block_send(CROSS, SIB2, p, at_sib) for p in (0, 1)]
    sib_relay = [block_send(RELAY, SIB2, p, at_sib) for p in (0, 1)]
    halo_up = send(HALO_LO, 0, edge.at[1], halo.at[0], at_up)
    halo_down = send(HALO_HI, 0, edge.at[0], halo.at[1], at_down)

    cross[0].start()
    transit_send.start()
    across[0].start()
    cross[1].start()
    sib.start()

    load_couple.wait()
    load_fields.wait()
    fields[...] = fields_in[...].astype(jnp.float32)

    def chosen(target):
        target = lax.rem(target + NBLK, NBLK)
        total = None
        for n in range(1, NNZ - 1):
            keep = (blocks_ref[0, n] == target).astype(jnp.float32)
            term = keep * couple[n].astype(jnp.float32)
            total = term if total is None else total + term
        return total

    def side_by_side(first, second):
        pair = jnp.concatenate([first, second], axis=-1)
        return pair.reshape(TERMS * MB, 2 * MB).astype(jnp.bfloat16)

    weights[:, 0:128] = side_by_side(couple[0].astype(jnp.float32), chosen(i + 1 - 2 * c))
    weights[:, 128:256] = side_by_side(
        couple[NNZ - 1].astype(jnp.float32), chosen(i + 2 - 4 * h)
    )
    weights[:, 256:384] = side_by_side(chosen(i - 2 + 4 * h), chosen(i - 1 + 2 * c))

    def multiply(part, first, last, fresh):
        @pl.loop(0, 8)
        def _(n):
            at = n // 4
            plane = 3 * at if part == 0 else 1 + at
            sy = lax.rem(n, 4) * 2
            depth = (last - first) * MB
            sides = [
                blocks[first:last, 2 * part + at, sy + k].reshape(depth, 128) for k in (0, 1)
            ]
            result = jnp.dot(
                weights[:, first * MB : last * MB],
                jnp.concatenate(sides, axis=1),
                preferred_element_type=jnp.float32,
            )
            for k in (0, 1):
                columns = slice(128 * k, 128 * (k + 1))
                term_d = result[0:MB, columns]
                row = plane * 4 + lax.rem(sy + k, 4)
                term_r = fields[pl.ds(row, 1), :] * result[MB : 2 * MB, columns]
                for t in range(1, K):
                    term_r = term_r + fields[pl.ds(16 * t + row, 1), :] * result[
                        (1 + t) * MB : (2 + t) * MB, columns
                    ]
                if fresh:
                    diff[1 + plane, sy + k] = term_d
                    react[plane, sy + k] = term_r
                else:
                    total = diff[1 + plane, sy + k] + term_d
                    diff[1 + plane, sy + k] = total
                    react[plane, sy + k] += term_r
                    if part == 0:
                        edge[at, sy + k] = total.astype(jnp.bfloat16)

    def pass_on(copies, yes, part):
        @pl.when(yes)
        def _():
            copies[part].start()

    cross[0].wait_recv()
    relay[0].start()
    pass_on(sib_cross, c == h, 0)
    transit_send.wait_recv()
    across[1].start()
    sib.wait_recv()
    across[0].wait_recv()
    multiply(0, OWN, RELAY, True)
    cross[1].wait_recv()
    relay[1].start()
    pass_on(sib_cross, c == h, 1)
    relay[0].wait_recv()
    pass_on(sib_relay, c != h, 0)
    sib_cross[0].wait_recv()
    multiply(0, RELAY, SIB2 + 1, False)
    halo_up.start()
    halo_down.start()
    across[1].wait_recv()
    multiply(1, OWN, RELAY, True)
    relay[1].wait_recv()
    pass_on(sib_relay, c != h, 1)
    sib_cross[1].wait_recv()
    multiply(1, RELAY, SIB2 + 1, False)
    halo_up.wait_recv()
    halo_down.wait_recv()

    @pl.loop(0, 8)
    def _(sy):
        diff[0, sy] = halo[0, sy].astype(jnp.float32)
        diff[5, sy] = halo[1, sy].astype(jnp.float32)

    for pos, plane in enumerate(PLANES):

        @pl.loop(0, 8)
        def _(sy, pos=pos, plane=plane):
            s = sy // 4
            yy = lax.rem(sy, 4)
            center = diff[1 + plane, sy]
            lap = diff[plane, sy] + diff[2 + plane, sy]
            lap = lap + diff[1 + plane, s * 4 + lax.rem(yy + 1, 4)]
            lap = lap + diff[1 + plane, s * 4 + lax.rem(yy + 3, 4)]
            lap = lap + pltpu.roll(center, 1, 1) + pltpu.roll(center, 127, 1)
            lap = lap - 6.0 * center
            mixed = mix_ref[s, 0] * blocks[OWN, pos, yy].astype(jnp.float32)
            mixed = mixed + mix_ref[s, 1] * blocks[OWN, pos, 4 + yy].astype(jnp.float32)
            start = s * 16 + plane * 4 + yy
            out_ref[pl.ds(start, MB, stride=STRIDE), :] = (
                react[plane, sy] - diffusivity_ref[s] * lap - mixed
            )

    for copy in (*cross, *relay, transit_send, *across, sib, *sib_cross, halo_up, halo_down):
        copy.wait_send()


def shards(
    section_field,
    base_field,
    prev_rate,
    block_list,
    coupling,
    diffusivity,
    reaction_fields,
    species_mix,
):
    rows, species, planes, depth, width = section_field.shape
    flat = rows * species * planes * depth
    lines = species * depth
    anywhere = pl.BlockSpec(memory_space=pl.ANY)
    scalars = pl.BlockSpec(memory_space=pltpu.SMEM)
    minus_rate = pl.pallas_call(
        kernel,
        name="galerkin",
        out_shape=jax.ShapeDtypeStruct((flat, width), jnp.float32),
        in_specs=[anywhere, anywhere, anywhere, scalars, scalars, scalars],
        out_specs=pl.BlockSpec(memory_space=pltpu.VMEM),
        scratch_shapes=[
            pltpu.VMEM((flat, width), jnp.bfloat16),
            pltpu.VMEM((flat, width), jnp.float32),
            pltpu.VMEM((NNZ, TERMS, MB, MB), jnp.bfloat16),
            pltpu.VMEM((K * planes * depth, width), jnp.bfloat16),
            pltpu.VMEM((K * planes * depth, width), jnp.float32),
            pltpu.VMEM((6, planes, lines, MB, width), jnp.bfloat16),
            pltpu.VMEM((2, lines, MB, width), jnp.bfloat16),
            pltpu.VMEM((TERMS * MB, 6 * MB), jnp.bfloat16),
            pltpu.VMEM((planes + 2, lines, MB, width), jnp.float32),
            pltpu.VMEM((planes, lines, MB, width), jnp.float32),
            pltpu.VMEM((2, lines, MB, width), jnp.bfloat16),
            pltpu.VMEM((2, lines, MB, width), jnp.bfloat16),
            pltpu.SemaphoreType.DMA((3,)),
            pltpu.SemaphoreType.DMA((9, 2)),
            pltpu.SemaphoreType.DMA((9, 2)),
        ],
        compiler_params=pltpu.CompilerParams(
            collective_id=0, has_side_effects=True, vmem_limit_bytes=32 * 1024 * 1024
        ),
        cost_estimate=pl.CostEstimate(
            flops=2 * TERMS * 6 * MB * MB * species * planes * depth * width,
            bytes_accessed=2**21,
            transcendentals=0,
        ),
    )(
        section_field.reshape(flat, width),
        coupling.reshape(NNZ, TERMS, MB, MB),
        reaction_fields.reshape(K * planes * depth, width),
        block_list,
        diffusivity,
        species_mix,
    )
    rate = -minus_rate.reshape(section_field.shape)
    next_field = (base_field.astype(jnp.float32) + half_step * (prev_rate + rate)).astype(
        jnp.bfloat16
    )
    return (rate, next_field)


def solution(mesh):
    placed = (
        P("mode", None, "gx", None, None),
        P("mode", None, "gx", None, None),
        P("mode", None, "gx", None, None),
        P("mode", None),
        P("mode", None, None, None, None),
        P(),
        P(None, "gx", None, None),
        P(),
    )
    return jax.shard_map(
        shards,
        mesh=mesh,
        in_specs=placed,
        out_specs=(P("mode", None, "gx", None, None), P("mode", None, "gx", None, None)),
        check_vma=False,
    )
```

time: 290 us -> 44.4 us (0.15); the launches traced: 285 us -> 43.8 us
  waiting for transfers between devices: 142 us -> 0 us
  matrix products: 47.1 us -> 0 us
  Pallas kernels: 0 us -> 36.6 us
  other arithmetic: 29.5 us -> 1.41 us
  loops' own time: 22.1 us -> 0 us
  local copies, waits for them, and re-layouts: 22.8 us -> 5.07 us
  between operations: 14.2 us -> 0.7 us
  starting transfers between devices: 6.45 us -> 0 us
    all_gather x2 -> x0, waiting for transfers between devices: 139 us -> none  [the longest x1 79.2 us: shards(): lap_piece = lax.all_gather(own_lap, 'mode', axis=0, tiled=True)]
    dot_general x25 -> x0, matrix products: 47.1 us -> none  [the longest x15 19.9 us: update(): jnp.dot(chosen[1 + term], field_block, preferred_element_type=jnp.float32)]
    pallas_call x0 -> x1, Pallas kernels: none -> 36.6 us  [shards(): pl.pallas_call(kernel, name='galerkin', out_shape=jax.ShapeDtypeStruct((f...]
    another operation x17 -> x0, loops' own time: 22.1 us -> none  [the longest x16 11.8 us: add_block(): return lax.cond(jnp.any(hits_all), update, unchanged, carry)]
    reduce_or x21 -> x0, other arithmetic: 14.2 us -> none  [the longest x16 11 us: add_block(): return lax.cond(jnp.any(hits_all), update, unchanged, carry)]
    reshape x12 -> x0, local copies, waits for them, and re-layouts: 7.84 us -> none  [the longest x1 2.02 us: shards(): reaction = reaction.reshape(rows_own, species, planes, depth, width)]
    dynamic_slice x5 -> x0, local copies, waits for them, and re-layouts: 7.83 us -> none  [fetch(): lax.dynamic_slice_in_dim(field_piece, offset, MB, 0).reshape(MB, cells)]
    ppermute x2 -> x0, starting transfers between devices: 6.38 us -> none  [the longest x1 5.38 us: padded_2(): lax.ppermute(head, axis, [((i + 1) % count, i) for i in range(count)])]
  transfers between devices with their start and end apart: 4 -> 0, of which waited for: 3 -> 0; matrix products, arithmetic and copies ran while one was open for 4% -> 0% of each run, Pallas kernels for 0% -> 0%
where the time goes in v1:
time: 44.4 us; the launch traced here: 43.8 us
  Pallas kernels  36.6 us (82%)
  local copies, waits for them, and re-layouts  5.07 us (11%)
  other arithmetic  1.41 us (3%)
  between operations  0.7 us (2%)
    pallas_call x1, Pallas kernels, shards(): pl.pallas_call(kernel, name='galerkin', out_shape=jax.ShapeDtypeStruct((f...  36.6 us
    unnamed x18, local copies, waits for them, and re-layouts  5.07 us
    convert_element_type x1, other arithmetic, shards(): (base_field.astype(jnp.float32) + half_step * (prev_rate + rate)).astype(...  1.34 us

profile of v1, /device:TPU:5, one launch (start us, length us, event | category | flops | bytes accessed | tf_op | source)
XLA Modules:
  0.0 43.8 jit_solution(11223508518474164259)
XLA Ops:
  0.6 0.0 copy-start.5
  0.6 0.0 copy-start.3
  0.7 0.0 copy-start.4
  0.7 0.6 %copy-done.5 = f32[2]{0:T(128)S(1)} copy-done((f32[2]{0:T(128)S(1)}, f32[2]{0:T(128)}, u32[]{:S(2)}) %copy-start.5) | copy-done | bytes 32
  1.3 0.0 copy-done.3
  1.3 0.0 copy-done.4
  1.3 0.0 copy-start
  1.3 1.0 %copy-done = bf16[64,2,4,4,128]{4,3,2,1,0:T(4,128)(2,1)S(1)} copy-done((bf16[64,2,4,4,128]{4,3,2,1,0:T(4,128)(2,1)S(1)}, bf16[64,2,4,4,128]{4,3,2,1,0:T(4,128)(2,1)}, u32[]{:S(2)}) %copy-start) | copy-done | bytes 524312
  2.4 0.0 copy-start.1
  2.4 1.0 %copy-done.1 = bf16[1,5,5,64,64]{4,3,2,1,0:T(8,128)(2,1)S(1)} copy-done((bf16[1,5,5,64,64]{4,3,2,1,0:T(8,128)(2,1)S(1)}, bf16[1,5,5,64,64]{4,3,2,1,0:T(8,128)(2,1)}, u32[]{:S(2)}) %copy-start.1) | copy-done | bytes 204824
  3.4 0.0 copy-start.2
  3.4 0.7 %copy-done.2 = bf16[4,4,4,128]{3,2,1,0:T(4,128)(2,1)S(1)} copy-done((bf16[4,4,4,128]{3,2,1,0:T(4,128)(2,1)S(1)}, bf16[4,4,4,128]{3,2,1,0:T(4,128)(2,1)}, u32[]{:S(2)}) %copy-start.2) | copy-done | bytes 16408
  4.1 36.6 %galerkin.1 = f32[2048,128]{1,0:T(8,128)S(1)} custom-call(bf16[2048,128]{1,0:T(8,128)(2,1)S(1)} %bitcast.4, bf16[5,5,64,64]{3,2,1,0:T(8,128)(2,1)S(1)} %bitcast.5, bf16[64,128]{1,0:T(8,128)(2,1)S(1)} %bitcast.6, s32[1,5]{1,0:T(1,128)S(1)} %copy-done.4, f32[2]{0:T(128)S(1)} %copy-done.5, f32[2,2]{1,0:T(2,128)S(1)} %copy-done.3), custom_call_target="tpu_custom_call" | custom-call | flops 1006632960 | bytes 2097152 | tf_op jit(solution)/shard_map/galerkin/pallas_call | solution.py:258
  40.7 0.0 copy-start.7
  40.8 0.0 copy-start.8
  40.8 0.1 neg.6
  40.8 0.0 copy-start.6
  40.9 1.5 %copy-done.7 = f32[64,2,4,4,128]{4,3,2,1,0:T(4,128)S(1)} copy-done((f32[64,2,4,4,128]{4,3,2,1,0:T(4,128)S(1)}, f32[64,2,4,4,128]{4,3,2,1,0:T(4,128)}, u32[]{:S(2)}) %copy-start.7) | copy-done | bytes 1048600
  42.4 0.1 copy-done.8
  42.5 1.3 %add_convert_fusion = bf16[64,2,4,4,128]{4,3,2,1,0:T(4,128)(2,1)} fusion(f32[64,2,4,4,128]{4,3,2,1,0:T(4,128)S(1)} %copy-done.7, f32[64,2,4,4,128]{4,3,2,1,0:T(4,128)S(1)} %bitcast.7, bf16[64,2,4,4,128]{4,3,2,1,0:T(4,128)(2,1)S(1)} %copy-done.8), kind=kLoop, calls=%fused_computation | loop fusion | flops 1310720 | bytes 3145728 | tf_op jit(solution)/shard_map/convert_element_type | solution.py:298
  43.8 0.0 copy-done.6
Async XLA Ops:
  0.6 0.7 %copy-start.5 = (f32[2]{0:T(128)S(1)}, f32[2]{0:T(128)}, u32[]{:S(2)}) copy-start(f32[2]{0:T(128)} %diffusivity_ref.1) | copy-start | bytes 28
  0.6 0.7 %copy-start.3 = (f32[2,2]{1,0:T(2,128)S(1)}, f32[2,2]{1,0:T(2,128)}, u32[]{:S(2)}) copy-start(f32[2,2]{1,0:T(2,128)} %mix_ref.1) | copy-start | bytes 52
  0.7 0.7 %copy-start.4 = (s32[1,5]{1,0:T(1,128)S(1)}, s32[1,5]{1,0:T(1,128)}, u32[]{:S(2)}) copy-start(s32[1,5]{1,0:T(1,128)} %blocks_ref.1) | copy-start | bytes 64
  1.3 1.0 %copy-start = (bf16[64,2,4,4,128]{4,3,2,1,0:T(4,128)(2,1)S(1)}, bf16[64,2,4,4,128]{4,3,2,1,0:T(4,128)(2,1)}, u32[]{:S(2)}) copy-start(bf16[64,2,4,4,128]{4,3,2,1,0:T(4,128)(2,1)} %param.8) | copy-start | bytes 1572868
  2.4 1.0 %copy-start.1 = (bf16[1,5,5,64,64]{4,3,2,1,0:T(8,128)(2,1)S(1)}, bf16[1,5,5,64,64]{4,3,2,1,0:T(8,128)(2,1)}, u32[]{:S(2)}) copy-start(bf16[1,5,5,64,64]{4,3,2,1,0:T(8,128)(2,1)} %param.12) | copy-start | bytes 614404
  3.4 0.7 %copy-start.2 = (bf16[4,4,4,128]{3,2,1,0:T(4,128)(2,1)S(1)}, bf16[4,4,4,128]{3,2,1,0:T(4,128)(2,1)}, u32[]{:S(2)}) copy-start(bf16[4,4,4,128]{3,2,1,0:T(4,128)(2,1)} %param.14) | copy-start | bytes 49156
  40.7 1.6 %copy-start.7 = (f32[64,2,4,4,128]{4,3,2,1,0:T(4,128)S(1)}, f32[64,2,4,4,128]{4,3,2,1,0:T(4,128)}, u32[]{:S(2)}) copy-start(f32[64,2,4,4,128]{4,3,2,1,0:T(4,128)} %param.10) | copy-start | bytes 3145732
  40.8 1.7 %copy-start.8 = (bf16[64,2,4,4,128]{4,3,2,1,0:T(4,128)(2,1)S(1)}, bf16[64,2,4,4,128]{4,3,2,1,0:T(4,128)(2,1)}, u32[]{:S(2)}) copy-start(bf16[64,2,4,4,128]{4,3,2,1,0:T(4,128)(2,1)} %param.9) | copy-start | bytes 1572868
  40.8 3.0 %copy-start.6 = (f32[2048,128]{1,0:T(8,128)}, f32[2048,128]{1,0:T(8,128)S(1)}, u32[]{:S(2)}) copy-start(f32[2048,128]{1,0:T(8,128)S(1)} %neg.6) | copy-start | bytes 3145732

commit v2 on v1

v2 whole, which is shorter than its diff:
```python
import jax
import jax.numpy as jnp
from jax import lax
from jax.sharding import PartitionSpec as P
import jax.experimental.pallas as pl
import jax.experimental.pallas.tpu as pltpu

MB = 64
NBLK = 16
K = 4
TERMS = 1 + K
NNZ = 5
MESH = pl.DeviceIdType.MESH

half_step = 0.25

OWN, SIB, ACROSS, CROSS, RELAY, SIB2 = range(6)
TRANSIT, HALO_LO, HALO_HI = 6, 7, 8
PLANES = (0, 3, 1, 2)
STRIDE = 32


def kernel(
    section_hbm,
    coupling_hbm,
    fields_hbm,
    list_hbm,
    diffusivity_hbm,
    mix_hbm,
    base_hbm,
    prev_hbm,
    out_ref,
    held_ref,
    list_ref,
    diffusivity_ref,
    mix_ref,
    base,
    native,
    wide,
    couple,
    fields_in,
    fields,
    blocks,
    transit,
    weights,
    diff,
    react,
    edge,
    halo,
    local_sem,
    send_sem,
    recv_sem,
    ready_sem,
    slabs_sem,
):
    g = lax.axis_index("gx")
    i = lax.axis_index("mode")
    y = i // 4
    h = lax.rem(i // 2, 2)
    c = lax.rem(i, 2)
    step = 1 - 2 * h

    def device(dy, hh, cc):
        return (g, lax.rem(y + dy + 4, 4) * 4 + hh * 2 + cc)

    at_cross = device(0, 1 - h, c)
    at_relay = device(step, h, c)
    at_back = device(-step, h, c)
    at_across = device(2, h, c)
    at_sib = device(0, h, 1 - c)
    at_up = (lax.rem(g + 1, 16), i)
    at_down = (lax.rem(g + 15, 16), i)

    def signal(sem, peer):
        pl.semaphore_signal(sem, inc=1, device_id=peer, device_id_type=MESH)

    load = pltpu.make_async_copy(section_hbm, native, local_sem.at[0])
    load.start()
    loads = [
        pltpu.make_async_copy(source, target, local_sem.at[1 + n])
        for n, (source, target) in enumerate(
            (
                (coupling_hbm, couple),
                (fields_hbm, fields_in),
                (list_hbm, list_ref),
                (diffusivity_hbm, diffusivity_ref),
                (mix_hbm, mix_ref),
                (base_hbm, base),
                (prev_hbm, held_ref),
            )
        )
    ]

    barrier = pltpu.get_barrier_semaphore()
    for peer in (device(0, 1 - h, 0), device(1, h, 0), device(3, h, 0), device(2, h, 0)):
        signal(barrier, peer)

    @pl.when(c == 1)
    def _():
        signal(barrier, at_sib)

    for copy in loads:
        copy.start()

    load.wait()

    @pl.loop(0, 8)
    def _(n):
        rows = pl.ds(pl.multiple_of(n * 256, 256), 256)
        wide[rows, :] = native[rows, :].astype(jnp.float32)

    for pos, plane in enumerate(PLANES):

        @pl.loop(0, 8)
        def _(sy, pos=pos, plane=plane):
            start = (sy // 4) * 16 + plane * 4 + lax.rem(sy, 4)
            blocks[OWN, pos, sy] = wide[pl.ds(start, MB, stride=STRIDE), :].astype(jnp.bfloat16)

    @pl.when(c == 0)
    def _():
        pl.semaphore_wait(barrier, 9)
        signal(ready_sem, at_sib)

    @pl.when(c == 1)
    def _():
        pl.semaphore_wait(ready_sem, 1)
        signal(barrier, at_up)
        signal(barrier, at_down)

    def send(kind, part, source, target, peer):
        return pltpu.make_async_remote_copy(
            src_ref=source,
            dst_ref=target,
            send_sem=send_sem.at[kind, part],
            recv_sem=recv_sem.at[kind, part],
            device_id=peer,
            device_id_type=MESH,
        )

    def block_send(source, target, pos, peer):
        return send(target, pos, blocks.at[source, pos], blocks.at[target, pos], peer)

    every = range(4)
    cross = [block_send(OWN, CROSS, p, at_cross) for p in every]
    relay = [block_send(CROSS, RELAY, p, at_relay) for p in every]
    back = [
        send(TRANSIT, p, blocks.at[OWN, p], transit.at[p - 2], at_back) for p in (2, 3)
    ]
    across = [
        send(ACROSS, 0, blocks.at[OWN, pl.ds(0, 2)], blocks.at[ACROSS, pl.ds(0, 2)], at_across)
    ] + [send(ACROSS, p, transit.at[p - 2], blocks.at[ACROSS, p], at_back) for p in (2, 3)]
    sib = send(SIB, 0, blocks.at[OWN], blocks.at[SIB], at_sib)
    sib_cross = [block_send(CROSS, SIB2, p, at_sib) for p in every]
    sib_relay = [block_send(RELAY, SIB2, p, at_sib) for p in every]
    halo_up = send(HALO_LO, 0, edge.at[1], halo.at[0], at_up)
    halo_down = send(HALO_HI, 0, edge.at[0], halo.at[1], at_down)

    cross[0].start()
    back[0].start()
    back[1].start()
    across[0].start()
    for p in (1, 2, 3):
        cross[p].start()
    sib.start()

    for copy in loads:
        copy.wait()
    fields[...] = fields_in[...].astype(jnp.float32)

    def chosen(target):
        target = lax.rem(target + NBLK, NBLK)
        total = None
        for n in range(1, NNZ - 1):
            keep = (list_ref[0, n] == target).astype(jnp.float32)
            term = keep * couple[n].astype(jnp.float32)
            total = term if total is None else total + term
        return total

    def side_by_side(first, second):
        pair = jnp.concatenate([first, second], axis=-1)
        return pair.reshape(TERMS * MB, 2 * MB).astype(jnp.bfloat16)

    weights[:, 0:128] = side_by_side(couple[0].astype(jnp.float32), chosen(i + 1 - 2 * c))
    weights[:, 128:256] = side_by_side(
        couple[NNZ - 1].astype(jnp.float32), chosen(i + 2 - 4 * h)
    )
    weights[:, 256:384] = side_by_side(chosen(i - 2 + 4 * h), chosen(i - 1 + 2 * c))

    @pl.loop(0, 8)
    def _(n):
        rows = pl.ds(pl.multiple_of(n * 256, 256), 256)
        held_ref[rows, :] = base[rows, :].astype(jnp.float32) + half_step * held_ref[rows, :]

    def multiply(pos, first, last):
        plane = PLANES[pos]
        fresh = first == OWN

        @pl.loop(0, 4, unroll=2)
        def _(n):
            sy = n * 2
            s = n // 2
            depth = (last - first) * MB
            sides = [blocks[first:last, pos, sy + k].reshape(depth, 128) for k in (0, 1)]
            result = jnp.dot(
                weights[:, first * MB : last * MB],
                jnp.concatenate(sides, axis=1),
                preferred_element_type=jnp.float32,
            )
            for k in (0, 1):
                columns = slice(128 * k, 128 * (k + 1))
                term_d = result[0:MB, columns]
                yy = lax.rem(sy, 4) + k
                row = plane * 4 + yy
                term_r = fields[pl.ds(row, 1), :] * result[MB : 2 * MB, columns]
                for t in range(1, K):
                    term_r = term_r + fields[pl.ds(16 * t + row, 1), :] * result[
                        (1 + t) * MB : (2 + t) * MB, columns
                    ]
                if fresh:
                    mixed = mix_ref[s, 0] * blocks[OWN, pos, yy].astype(jnp.float32)
                    mixed = mixed + mix_ref[s, 1] * blocks[OWN, pos, 4 + yy].astype(jnp.float32)
                    diff[1 + plane, sy + k] = term_d
                    react[plane, sy + k] = term_r - mixed
                else:
                    total = diff[1 + plane, sy + k] + term_d
                    diff[1 + plane, sy + k] = total
                    react[plane, sy + k] += term_r
                    if pos < 2:
                        edge[pos, sy + k] = total.astype(jnp.bfloat16)

    def in_plane(plane, sy):
        s4 = (sy // 4) * 4
        center = diff[1 + plane, sy]
        lap = diff[1 + plane, s4 + (sy + 1) % 4] + diff[1 + plane, s4 + (sy + 3) % 4]
        lap = lap + (pltpu.roll(center, 1, 1) + pltpu.roll(center, 127, 1))
        return lap - 6.0 * center

    def pass_on(copies, yes, p):
        @pl.when(yes)
        def _():
            copies[p].start()

    def take_cross(p):
        cross[p].wait_recv()
        relay[p].start()
        pass_on(sib_cross, c == h, p)

    def take_relay(p):
        relay[p].wait_recv()
        pass_on(sib_relay, c != h, p)

    take_cross(0)
    take_cross(1)
    for n in (0, 1):
        back[n].wait_recv()
        across[1 + n].start()
    sib.wait_recv()
    across[0].wait_recv()
    multiply(0, OWN, RELAY)
    take_cross(2)
    take_relay(0)
    multiply(1, OWN, RELAY)
    take_cross(3)
    take_relay(1)
    for p in (0, 1):
        sib_cross[p].wait_recv()
        multiply(p, RELAY, SIB2 + 1)

    @pl.when(c == 1)
    def _():
        pl.semaphore_wait(barrier, 2)
        signal(slabs_sem, at_sib)

    @pl.when(c == 0)
    def _():
        pl.semaphore_wait(slabs_sem, 1)

    halo_up.start()
    halo_down.start()

    for plane in (0, 3):
        for sy in range(8):
            react[plane, sy] -= diffusivity_ref[sy // 4] * in_plane(plane, sy)

    for n in (0, 1):
        across[1 + n].wait_recv()
        multiply(2 + n, OWN, RELAY)
    for p in (2, 3):
        take_relay(p)
        sib_cross[p].wait_recv()
        multiply(p, RELAY, SIB2 + 1)
    halo_up.wait_recv()
    halo_down.wait_recv()

    for sy in range(8):
        scale = diffusivity_ref[sy // 4]
        d = [diff[1 + plane, sy] for plane in range(4)]
        low = halo[0, sy].astype(jnp.float32)
        high = halo[1, sy].astype(jnp.float32)
        parts = (
            low + d[1],
            d[0] + d[2] + in_plane(1, sy),
            d[1] + d[3] + in_plane(2, sy),
            d[2] + high,
        )
        for plane in range(4):
            start = (sy // 4) * 16 + plane * 4 + sy % 4
            out_ref[pl.ds(start, MB, stride=STRIDE), :] = (
                react[plane, sy] - scale * parts[plane]
            )

    for copy in (*cross, *relay, *back, *across, sib, *sib_cross, halo_up, halo_down):
        copy.wait_send()


def shards(
    section_field,
    base_field,
    prev_rate,
    block_list,
    coupling,
    diffusivity,
    reaction_fields,
    species_mix,
):
    rows, species, planes, depth, width = section_field.shape
    flat = rows * species * planes * depth
    lines = species * depth
    in_hbm = pl.BlockSpec(memory_space=pltpu.HBM)
    in_vmem = pl.BlockSpec(memory_space=pltpu.VMEM)
    minus_rate, held = pl.pallas_call(
        kernel,
        name="galerkin",
        out_shape=(
            pltpu.VMEM((flat, width), jnp.float32),
            pltpu.VMEM((flat, width), jnp.float32),
        ),
        in_specs=[in_hbm] * 8,
        out_specs=(in_vmem, in_vmem),
        scratch_shapes=[
            pltpu.SMEM(block_list.shape, block_list.dtype),
            pltpu.SMEM(diffusivity.shape, diffusivity.dtype),
            pltpu.SMEM(species_mix.shape, species_mix.dtype),
            pltpu.VMEM((flat, width), jnp.bfloat16),
            pltpu.VMEM((flat, width), jnp.bfloat16),
            pltpu.VMEM((flat, width), jnp.float32),
            pltpu.VMEM((NNZ, TERMS, MB, MB), jnp.bfloat16),
            pltpu.VMEM((K * planes * depth, width), jnp.bfloat16),
            pltpu.VMEM((K * planes * depth, width), jnp.float32),
            pltpu.VMEM((6, planes, lines, MB, width), jnp.bfloat16),
            pltpu.VMEM((2, lines, MB, width), jnp.bfloat16),
            pltpu.VMEM((TERMS * MB, 6 * MB), jnp.bfloat16),
            pltpu.VMEM((planes + 2, lines, MB, width), jnp.float32),
            pltpu.VMEM((planes, lines, MB, width), jnp.float32),
            pltpu.VMEM((2, lines, MB, width), jnp.bfloat16),
            pltpu.VMEM((2, lines, MB, width), jnp.bfloat16),
            pltpu.SemaphoreType.DMA((8,)),
            pltpu.SemaphoreType.DMA((9, 4)),
            pltpu.SemaphoreType.DMA((9, 4)),
            pltpu.SemaphoreType.REGULAR,
            pltpu.SemaphoreType.REGULAR,
        ],
        compiler_params=pltpu.CompilerParams(
            collective_id=0, has_side_effects=True, vmem_limit_bytes=57 * 1024 * 1024
        ),
        cost_estimate=pl.CostEstimate(
            flops=2 * TERMS * 6 * MB * MB * species * planes * depth * width,
            bytes_accessed=2**21,
            transcendentals=0,
        ),
    )(
        section_field.reshape(flat, width),
        coupling.reshape(NNZ, TERMS, MB, MB),
        reaction_fields.reshape(K * planes * depth, width),
        block_list,
        diffusivity,
        species_mix,
        base_field.reshape(flat, width),
        prev_rate.reshape(flat, width),
    )
    rate = -minus_rate
    next_field = (held - half_step * minus_rate).astype(jnp.bfloat16)
    return (rate.reshape(section_field.shape), next_field.reshape(section_field.shape))


def solution(mesh):
    placed = (
        P("mode", None, "gx", None, None),
        P("mode", None, "gx", None, None),
        P("mode", None, "gx", None, None),
        P("mode", None),
        P("mode", None, None, None, None),
        P(),
        P(None, "gx", None, None),
        P(),
    )
    return jax.shard_map(
        shards,
        mesh=mesh,
        in_specs=placed,
        out_specs=(P("mode", None, "gx", None, None), P("mode", None, "gx", None, None)),
        check_vma=False,
    )
```

time: 44.4 us -> 35.8 us (0.81)
  local copies, waits for them, and re-layouts: 5.07 us -> 0 us
  Pallas kernels: 36.6 us -> 33.4 us
    unnamed x18 -> x0, local copies, waits for them, and re-layouts: 5.07 us -> none
    pallas_call x1, Pallas kernels: 36.6 us -> 33.4 us  [shards(): pl.pallas_call(kernel, name='galerkin', out_shape=(pltpu.VMEM((flat, widt...]
where the time goes in v2:
time: 35.8 us; the launch traced here: 35.3 us
  Pallas kernels  33.4 us (93%)
  other arithmetic  1.3 us (4%)
  between operations  0.64 us (2%)
    pallas_call x1, Pallas kernels, shards(): pl.pallas_call(kernel, name='galerkin', out_shape=(pltpu.VMEM((flat, widt...  33.4 us
    convert_element_type x1, other arithmetic, shards(): next_field = (held - half_step * minus_rate).astype(jnp.bfloat16)  1.3 us

profile of v2, /device:TPU:5, one launch (start us, length us, event | category | flops | bytes accessed | tf_op | source)
XLA Modules:
  0.0 35.3 jit_solution(6410219796312912049)
XLA Ops:
  0.6 33.4 %galerkin.1 = (f32[2048,128]{1,0:T(8,128)S(1)}, f32[2048,128]{1,0:T(8,128)S(1)}) custom-call(bf16[2048,128]{1,0:T(8,128)(2,1)} %bitcast.10, bf16[5,5,64,64]{3,2,1,0:T(8,128)(2,1)} %bitcast.12, bf16[64,128]{1,0:T(8,128)(2,1)} %bitcast.13, s32[1,5]{1,0:T(1,128)} %list_hbm.1, f32[2]{0:T(128)} %diffusivity_hbm.1, f32[2,2]{1,0:T(2,128)} %mix_hbm.1, ...), custom_call_target="tpu_custom_call" | custom-call | flops 1006632960 | bytes 2097152 | tf_op jit(solution)/shard_map/galerkin/pallas_call | solution.py:331
  34.0 1.3 %subtract_convert_fusion = (bf16[2048,128]{1,0:T(8,128)(2,1)}, f32[2048,128]{1,0:T(8,128)}) fusion(f32[2048,128]{1,0:T(8,128)S(1)} %get-tuple-element.5, f32[2048,128]{1,0:T(8,128)S(1)} %get-tuple-element.4), kind=kLoop, calls=%fused_computation | loop fusion | flops 1048576 | bytes 3670016 | tf_op jit(solution)/shard_map/convert_element_type | solution.py:382

commit v3 on v2

--- a/solution.py
+++ b/solution.py
@@ -16,7 +16,8 @@
 
 OWN, SIB, ACROSS, CROSS, RELAY, SIB2 = range(6)
 TRANSIT, HALO_LO, HALO_HI = 6, 7, 8
-PLANES = (0, 3, 1, 2)
+PLANES = (3, 0, 1, 2)
+PIECE = 512
 STRIDE = 32
 
 
@@ -47,6 +48,7 @@
     react,
     edge,
     halo,
+    own_sem,
     local_sem,
     send_sem,
     recv_sem,
@@ -74,10 +76,15 @@
     def signal(sem, peer):
         pl.semaphore_signal(sem, inc=1, device_id=peer, device_id_type=MESH)
 
-    load = pltpu.make_async_copy(section_hbm, native, local_sem.at[0])
-    load.start()
+    pieces = [pl.ds(n * PIECE, PIECE) for n in range(section_hbm.shape[0] // PIECE)]
+    own = [
+        pltpu.make_async_copy(section_hbm.at[rows], native.at[rows], own_sem.at[n])
+        for n, rows in enumerate(pieces)
+    ]
+    for copy in own:
+        copy.start()
     loads = [
-        pltpu.make_async_copy(source, target, local_sem.at[1 + n])
+        pltpu.make_async_copy(source, target, local_sem.at[n])
         for n, (source, target) in enumerate(
             (
                 (coupling_hbm, couple),
@@ -102,19 +109,17 @@
     for copy in loads:
         copy.start()
 
-    load.wait()
-
-    @pl.loop(0, 8)
-    def _(n):
-        rows = pl.ds(pl.multiple_of(n * 256, 256), 256)
+    for copy, rows in zip(own, pieces):
+        copy.wait()
         wide[rows, :] = native[rows, :].astype(jnp.float32)
 
-    for pos, plane in enumerate(PLANES):
-
-        @pl.loop(0, 8)
-        def _(sy, pos=pos, plane=plane):
-            start = (sy // 4) * 16 + plane * 4 + lax.rem(sy, 4)
+    def arrange(pos):
+        for sy in range(8):
+            start = (sy // 4) * 16 + PLANES[pos] * 4 + sy % 4
             blocks[OWN, pos, sy] = wide[pl.ds(start, MB, stride=STRIDE), :].astype(jnp.bfloat16)
+
+    arrange(0)
+    arrange(1)
 
     @pl.when(c == 0)
     def _():
@@ -146,21 +151,25 @@
     back = [
         send(TRANSIT, p, blocks.at[OWN, p], transit.at[p - 2], at_back) for p in (2, 3)
     ]
-    across = [
-        send(ACROSS, 0, blocks.at[OWN, pl.ds(0, 2)], blocks.at[ACROSS, pl.ds(0, 2)], at_across)
-    ] + [send(ACROSS, p, transit.at[p - 2], blocks.at[ACROSS, p], at_back) for p in (2, 3)]
+    across = [block_send(OWN, ACROSS, p, at_across) for p in (0, 1)] + [
+        send(ACROSS, p, transit.at[p - 2], blocks.at[ACROSS, p], at_back) for p in (2, 3)
+    ]
     sib = send(SIB, 0, blocks.at[OWN], blocks.at[SIB], at_sib)
     sib_cross = [block_send(CROSS, SIB2, p, at_sib) for p in every]
     sib_relay = [block_send(RELAY, SIB2, p, at_sib) for p in every]
-    halo_up = send(HALO_LO, 0, edge.at[1], halo.at[0], at_up)
-    halo_down = send(HALO_HI, 0, edge.at[0], halo.at[1], at_down)
+    halo_up = send(HALO_LO, 0, edge.at[0], halo.at[0], at_up)
+    halo_down = send(HALO_HI, 0, edge.at[1], halo.at[1], at_down)
 
     cross[0].start()
+    across[0].start()
+    cross[1].start()
+    across[1].start()
+    arrange(2)
+    cross[2].start()
     back[0].start()
+    arrange(3)
+    cross[3].start()
     back[1].start()
-    across[0].start()
-    for p in (1, 2, 3):
-        cross[p].start()
     sib.start()
 
     for copy in loads:
@@ -249,65 +258,71 @@
         relay[p].wait_recv()
         pass_on(sib_relay, c != h, p)
 
+    def slab_entered():
+        @pl.when(c == 1)
+        def _():
+            pl.semaphore_wait(barrier, 2)
+            signal(slabs_sem, at_sib)
+
+        @pl.when(c == 0)
+        def _():
+            pl.semaphore_wait(slabs_sem, 1)
+
+    def late(pos):
+        take_relay(pos)
+        sib_cross[pos].wait_recv()
+        multiply(pos, RELAY, SIB2 + 1)
+
+    def lessen(plane, others):
+        for sy in range(8):
+            part = in_plane(plane, sy)
+            for other in others:
+                part = part + diff[1 + other, sy]
+            react[plane, sy] -= diffusivity_ref[sy // 4] * part
+
+    def finish(plane, sy, part):
+        start = (sy // 4) * 16 + plane * 4 + sy % 4
+        out_ref[pl.ds(start, MB, stride=STRIDE), :] = (
+            react[plane, sy] - diffusivity_ref[sy // 4] * part
+        )
+
     take_cross(0)
-    take_cross(1)
-    for n in (0, 1):
-        back[n].wait_recv()
-        across[1 + n].start()
     sib.wait_recv()
     across[0].wait_recv()
     multiply(0, OWN, RELAY)
+    take_cross(1)
+    back[0].wait_recv()
+    across[2].start()
+    late(0)
+    slab_entered()
+    halo_up.start()
+    across[1].wait_recv()
     take_cross(2)
-    take_relay(0)
     multiply(1, OWN, RELAY)
+    back[1].wait_recv()
+    across[3].start()
+    late(1)
+    halo_down.start()
     take_cross(3)
-    take_relay(1)
-    for p in (0, 1):
-        sib_cross[p].wait_recv()
-        multiply(p, RELAY, SIB2 + 1)
-
-    @pl.when(c == 1)
-    def _():
-        pl.semaphore_wait(barrier, 2)
-        signal(slabs_sem, at_sib)
-
-    @pl.when(c == 0)
-    def _():
-        pl.semaphore_wait(slabs_sem, 1)
-
-    halo_up.start()
-    halo_down.start()
-
-    for plane in (0, 3):
-        for sy in range(8):
-            react[plane, sy] -= diffusivity_ref[sy // 4] * in_plane(plane, sy)
-
-    for n in (0, 1):
-        across[1 + n].wait_recv()
-        multiply(2 + n, OWN, RELAY)
-    for p in (2, 3):
-        take_relay(p)
-        sib_cross[p].wait_recv()
-        multiply(p, RELAY, SIB2 + 1)
+    across[2].wait_recv()
+    multiply(2, OWN, RELAY)
+    lessen(3, ())
+    lessen(0, ())
+    late(2)
+    lessen(1, (0,))
+    across[3].wait_recv()
+    multiply(3, OWN, RELAY)
+    late(3)
+    for sy in range(8):
+        inner = diff[3, sy]
+        finish(1, sy, inner)
+        finish(2, sy, in_plane(2, sy) + (diff[2, sy] + diff[4, sy]))
+    halo_down.wait_recv()
+    for sy in range(8):
+        finish(3, sy, diff[3, sy] + halo[1, sy].astype(jnp.float32))
     halo_up.wait_recv()
-    halo_down.wait_recv()
-
     for sy in range(8):
-        scale = diffusivity_ref[sy // 4]
-        d = [diff[1 + plane, sy] for plane in range(4)]
-        low = halo[0, sy].astype(jnp.float32)
-        high = halo[1, sy].astype(jnp.float32)
-        parts = (
-            low + d[1],
-            d[0] + d[2] + in_plane(1, sy),
-            d[1] + d[3] + in_plane(2, sy),
-            d[2] + high,
-        )
-        for plane in range(4):
-            start = (sy // 4) * 16 + plane * 4 + sy % 4
-            out_ref[pl.ds(start, MB, stride=STRIDE), :] = (
-                react[plane, sy] - scale * parts[plane]
-            )
+        finish(0, sy, diff[2, sy] + halo[0, sy].astype(jnp.float32))
 
     for copy in (*cross, *relay, *back, *across, sib, *sib_cross, halo_up, halo_down):
         copy.wait_send()
@@ -354,7 +369,8 @@
             pltpu.VMEM((planes, lines, MB, width), jnp.float32),
             pltpu.VMEM((2, lines, MB, width), jnp.bfloat16),
             pltpu.VMEM((2, lines, MB, width), jnp.bfloat16),
-            pltpu.SemaphoreType.DMA((8,)),
+            pltpu.SemaphoreType.DMA((flat // PIECE,)),
+            pltpu.SemaphoreType.DMA((7,)),
             pltpu.SemaphoreType.DMA((9, 4)),
             pltpu.SemaphoreType.DMA((9, 4)),
             pltpu.SemaphoreType.REGULAR,

time: 35.8 us -> 30.5 us (0.85)
  the two profiles are of different devices: /device:TPU:5 before, /device:TPU:103 now
where the time goes in v3:
time: 30.5 us; the launch traced here: 30.4 us
  Pallas kernels  28.4 us (93%)
  other arithmetic  1.3 us (4%)
  between operations  0.64 us (2%)
    pallas_call x1, Pallas kernels, shards(): pl.pallas_call(kernel, name='galerkin', out_shape=(pltpu.VMEM((flat, widt...  28.4 us
    convert_element_type x1, other arithmetic, shards(): next_field = (held - half_step * minus_rate).astype(jnp.bfloat16)  1.3 us

profile of v3, /device:TPU:103, one launch (start us, length us, event | category | flops | bytes accessed | tf_op | source)
XLA Modules:
  0.0 30.4 jit_solution(11339486689423301139)
XLA Ops:
  0.6 28.4 %galerkin.1 = (f32[2048,128]{1,0:T(8,128)S(1)}, f32[2048,128]{1,0:T(8,128)S(1)}) custom-call(bf16[2048,128]{1,0:T(8,128)(2,1)} %bitcast.10, bf16[5,5,64,64]{3,2,1,0:T(8,128)(2,1)} %bitcast.12, bf16[64,128]{1,0:T(8,128)(2,1)} %bitcast.13, s32[1,5]{1,0:T(1,128)} %list_hbm.1, f32[2]{0:T(128)} %diffusivity_hbm.1, f32[2,2]{1,0:T(2,128)} %mix_hbm.1, ...), custom_call_target="tpu_custom_call" | custom-call | flops 1006632960 | bytes 2097152 | tf_op jit(solution)/shard_map/galerkin/pallas_call | solution.py:346
  29.1 1.3 %subtract_convert_fusion = (bf16[2048,128]{1,0:T(8,128)(2,1)}, f32[2048,128]{1,0:T(8,128)}) fusion(f32[2048,128]{1,0:T(8,128)S(1)} %get-tuple-element.5, f32[2048,128]{1,0:T(8,128)S(1)} %get-tuple-element.4), kind=kLoop, calls=%fused_computation | loop fusion | flops 1048576 | bytes 3670016 | tf_op jit(solution)/shard_map/convert_element_type | solution.py:398

commit v4 on v3

--- a/solution.py
+++ b/solution.py
@@ -53,6 +53,7 @@
     send_sem,
     recv_sem,
     ready_sem,
+    gather_sem,
     slabs_sem,
 ):
     g = lax.axis_index("gx")
@@ -98,13 +99,25 @@
         )
     ]
 
+    first = y == 0
+    second = y == 1
     barrier = pltpu.get_barrier_semaphore()
-    for peer in (device(0, 1 - h, 0), device(1, h, 0), device(3, h, 0), device(2, h, 0)):
-        signal(barrier, peer)
-
-    @pl.when(c == 1)
-    def _():
+
+    @pl.when(jnp.logical_not(first))
+    def _():
+        signal(barrier, at_cross)
         signal(barrier, at_sib)
+
+    for dy in (1, 2, 3):
+
+        @pl.when(lax.rem(y + dy, 4) != 0)
+        def _(dy=dy):
+            signal(barrier, device(dy, h, c))
+
+    @pl.when(first)
+    def _():
+        signal(barrier, device(1, 1 - h, c))
+        signal(barrier, device(1, h, 1 - c))
 
     for copy in loads:
         copy.start()
@@ -121,16 +134,19 @@
     arrange(0)
     arrange(1)
 
-    @pl.when(c == 0)
-    def _():
-        pl.semaphore_wait(barrier, 9)
-        signal(ready_sem, at_sib)
-
-    @pl.when(c == 1)
+    @pl.when(second)
+    def _():
+        pl.semaphore_wait(barrier, 7)
+        signal(ready_sem, device(3, h, c))
+
+    @pl.when(y > 1)
+    def _():
+        pl.semaphore_wait(barrier, 5)
+        signal(gather_sem, device(4 - y, h, c))
+
+    @pl.when(first)
     def _():
         pl.semaphore_wait(ready_sem, 1)
-        signal(barrier, at_up)
-        signal(barrier, at_down)
 
     def send(kind, part, source, target, peer):
         return pltpu.make_async_remote_copy(
@@ -162,15 +178,21 @@
 
     cross[0].start()
     across[0].start()
+    arrange(2)
+    back[0].start()
     cross[1].start()
     across[1].start()
-    arrange(2)
+    arrange(3)
+    back[1].start()
     cross[2].start()
-    back[0].start()
-    arrange(3)
     cross[3].start()
-    back[1].start()
     sib.start()
+
+    @pl.when(first)
+    def _():
+        pl.semaphore_wait(gather_sem, 2)
+        signal(barrier, at_up)
+        signal(barrier, at_down)
 
     for copy in loads:
         copy.wait()
@@ -197,14 +219,14 @@
 
     @pl.loop(0, 8)
     def _(n):
-        rows = pl.ds(pl.multiple_of(n * 256, 256), 256)
-        held_ref[rows, :] = base[rows, :].astype(jnp.float32) + half_step * held_ref[rows, :]
+        rows = pl.ds(n * 8, 8)
+        held_ref[rows] = base[rows].astype(jnp.float32) + half_step * held_ref[rows]
 
     def multiply(pos, first, last):
         plane = PLANES[pos]
         fresh = first == OWN
 
-        @pl.loop(0, 4, unroll=2)
+        @pl.loop(0, 4, unroll=4)
         def _(n):
             sy = n * 2
             s = n // 2
@@ -258,18 +280,7 @@
         relay[p].wait_recv()
         pass_on(sib_relay, c != h, p)
 
-    def slab_entered():
-        @pl.when(c == 1)
-        def _():
-            pl.semaphore_wait(barrier, 2)
-            signal(slabs_sem, at_sib)
-
-        @pl.when(c == 0)
-        def _():
-            pl.semaphore_wait(slabs_sem, 1)
-
     def late(pos):
-        take_relay(pos)
         sib_cross[pos].wait_recv()
         multiply(pos, RELAY, SIB2 + 1)
 
@@ -280,49 +291,86 @@
                 part = part + diff[1 + other, sy]
             react[plane, sy] -= diffusivity_ref[sy // 4] * part
 
-    def finish(plane, sy, part):
-        start = (sy // 4) * 16 + plane * 4 + sy % 4
-        out_ref[pl.ds(start, MB, stride=STRIDE), :] = (
-            react[plane, sy] - diffusivity_ref[sy // 4] * part
-        )
+    def finish():
+        @pl.loop(0, MB // 16, unroll=4)
+        def _(n):
+            rows = pl.ds(pl.multiple_of(16 * n, 16), 16)
+
+            def at(plane, sy):
+                return diff[1 + plane, sy, rows, :]
+
+            def in_plane_rows(plane, sy):
+                s4 = (sy // 4) * 4
+                center = at(plane, sy)
+                lap = at(plane, s4 + (sy + 1) % 4) + at(plane, s4 + (sy + 3) % 4)
+                lap = lap + (pltpu.roll(center, 1, 1) + pltpu.roll(center, 127, 1))
+                return lap - 6.0 * center
+
+            for s in range(2):
+                for pair in range(2):
+                    lines = []
+                    for plane in (2 * pair, 2 * pair + 1):
+                        for sy in range(4 * s, 4 * s + 4):
+                            if plane == 0:
+                                part = at(1, sy) + halo[0, sy, rows, :].astype(jnp.float32)
+                            elif plane == 1:
+                                part = at(2, sy)
+                            elif plane == 2:
+                                part = in_plane_rows(2, sy) + (at(1, sy) + at(3, sy))
+                            else:
+                                part = at(2, sy) + halo[1, sy, rows, :].astype(jnp.float32)
+                            lines.append(
+                                react[plane, sy, rows, :] - diffusivity_ref[s] * part
+                            )
+                    out_ref[rows, pl.ds(8 * (2 * s + pair), 8), :] = jnp.swapaxes(
+                        jnp.stack(lines, axis=0), 0, 1
+                    )
 
     take_cross(0)
+    take_cross(1)
+    back[0].wait_recv()
+    across[2].start()
     sib.wait_recv()
     across[0].wait_recv()
     multiply(0, OWN, RELAY)
-    take_cross(1)
-    back[0].wait_recv()
-    across[2].start()
+    take_relay(0)
+
+    @pl.when(first)
+    def _():
+        pl.semaphore_wait(barrier, 2)
+        for dy in (1, 2, 3):
+            signal(slabs_sem, device(dy, h, c))
+
     late(0)
-    slab_entered()
+
+    @pl.when(jnp.logical_not(first))
+    def _():
+        pl.semaphore_wait(slabs_sem, 1)
+
     halo_up.start()
+    take_cross(2)
     across[1].wait_recv()
-    take_cross(2)
     multiply(1, OWN, RELAY)
     back[1].wait_recv()
     across[3].start()
+    take_cross(3)
+    take_relay(1)
+    lessen(3, ())
     late(1)
     halo_down.start()
-    take_cross(3)
+    lessen(0, ())
     across[2].wait_recv()
     multiply(2, OWN, RELAY)
-    lessen(3, ())
-    lessen(0, ())
+    take_relay(2)
     late(2)
     lessen(1, (0,))
     across[3].wait_recv()
     multiply(3, OWN, RELAY)
+    take_relay(3)
     late(3)
-    for sy in range(8):
-        inner = diff[3, sy]
-        finish(1, sy, inner)
-        finish(2, sy, in_plane(2, sy) + (diff[2, sy] + diff[4, sy]))
     halo_down.wait_recv()
-    for sy in range(8):
-        finish(3, sy, diff[3, sy] + halo[1, sy].astype(jnp.float32))
     halo_up.wait_recv()
-    for sy in range(8):
-        finish(0, sy, diff[2, sy] + halo[0, sy].astype(jnp.float32))
+    finish()
 
     for copy in (*cross, *relay, *back, *across, sib, *sib_cross, halo_up, halo_down):
         copy.wait_send()
@@ -347,8 +395,8 @@
         kernel,
         name="galerkin",
         out_shape=(
-            pltpu.VMEM((flat, width), jnp.float32),
-            pltpu.VMEM((flat, width), jnp.float32),
+            pltpu.VMEM((rows, STRIDE, width), jnp.float32),
+            pltpu.VMEM((rows, STRIDE, width), jnp.float32),
         ),
         in_specs=[in_hbm] * 8,
         out_specs=(in_vmem, in_vmem),
@@ -356,7 +404,7 @@
             pltpu.SMEM(block_list.shape, block_list.dtype),
             pltpu.SMEM(diffusivity.shape, diffusivity.dtype),
             pltpu.SMEM(species_mix.shape, species_mix.dtype),
-            pltpu.VMEM((flat, width), jnp.bfloat16),
+            pltpu.VMEM((rows, STRIDE, width), jnp.bfloat16),
             pltpu.VMEM((flat, width), jnp.bfloat16),
             pltpu.VMEM((flat, width), jnp.float32),
             pltpu.VMEM((NNZ, TERMS, MB, MB), jnp.bfloat16),
@@ -375,6 +423,7 @@
             pltpu.SemaphoreType.DMA((9, 4)),
             pltpu.SemaphoreType.REGULAR,
             pltpu.SemaphoreType.REGULAR,
+            pltpu.SemaphoreType.REGULAR,
         ],
         compiler_params=pltpu.CompilerParams(
             collective_id=0, has_side_effects=True, vmem_limit_bytes=57 * 1024 * 1024
@@ -391,8 +440,8 @@
         block_list,
         diffusivity,
         species_mix,
-        base_field.reshape(flat, width),
-        prev_rate.reshape(flat, width),
+        base_field.reshape(rows, STRIDE, width),
+        prev_rate.reshape(rows, STRIDE, width),
     )
     rate = -minus_rate
     next_field = (held - half_step * minus_rate).astype(jnp.bfloat16)

time: 30.5 us -> 29.6 us (0.970)
  the two profiles are of different devices: /device:TPU:103 before, /device:TPU:199 now
where the time goes in v4:
time: 29.6 us; the launch traced here: 29.5 us
  Pallas kernels  27.4 us (93%)
  other arithmetic  1.38 us (5%)
  between operations  0.64 us (2%)
    pallas_call x1, Pallas kernels, shards(): pl.pallas_call(kernel, name='galerkin', out_shape=(pltpu.VMEM((rows, STRI...  27.4 us
    convert_element_type x1, other arithmetic, shards(): next_field = (held - half_step * minus_rate).astype(jnp.bfloat16)  1.38 us

profile of v4, /device:TPU:199, one launch (start us, length us, event | category | flops | bytes accessed | tf_op | source)
XLA Modules:
  0.0 29.5 jit_solution(4303862858053510946)
XLA Ops:
  0.6 27.4 %galerkin.1 = (f32[64,32,128]{2,1,0:T(8,128)S(1)}, f32[64,32,128]{2,1,0:T(8,128)S(1)}) custom-call(bf16[2048,128]{1,0:T(8,128)(2,1)} %bitcast.10, bf16[5,5,64,64]{3,2,1,0:T(8,128)(2,1)} %bitcast.12, bf16[64,128]{1,0:T(8,128)(2,1)} %bitcast.13, s32[1,5]{1,0:T(1,128)} %list_hbm.1, f32[2]{0:T(128)} %diffusivity_hbm.1, f32[2,2]{1,0:T(2,128)} %mix_hbm.1, ...), custom_call_target="tpu_custom_call" | custom-call | flops 1006632960 | bytes 2097152 | tf_op jit(solution)/shard_map/galerkin/pallas_call | solution.py:394
  28.1 1.4 %subtract_convert_fusion = (bf16[64,32,128]{2,1,0:T(8,128)(2,1)}, f32[64,32,128]{2,1,0:T(8,128)}) fusion(f32[64,32,128]{2,1,0:T(8,128)S(1)} %get-tuple-element.5, f32[64,32,128]{2,1,0:T(8,128)S(1)} %get-tuple-element.4), kind=kLoop, calls=%fused_computation | loop fusion | flops 1048576 | bytes 3670016 | tf_op jit(solution)/shard_map/convert_element_type | solution.py:447

commit v5 on v4

--- a/solution.py
+++ b/solution.py
@@ -71,8 +71,12 @@
     at_back = device(-step, h, c)
     at_across = device(2, h, c)
     at_sib = device(0, h, 1 - c)
-    at_up = (lax.rem(g + 1, 16), i)
-    at_down = (lax.rem(g + 15, 16), i)
+    flip = 1 - lax.rem(g, 2)
+    at_up = (lax.rem(g + 17 - 2 * flip, 16), i)
+    at_down = (lax.rem(g + 15 + 2 * flip, 16), i)
+
+    def plane_of(plane):
+        return plane + flip * (3 - 2 * plane)
 
     def signal(sem, peer):
         pl.semaphore_signal(sem, inc=1, device_id=peer, device_id_type=MESH)
@@ -128,7 +132,7 @@
 
     def arrange(pos):
         for sy in range(8):
-            start = (sy // 4) * 16 + PLANES[pos] * 4 + sy % 4
+            start = (sy // 4) * 16 + plane_of(PLANES[pos]) * 4 + sy % 4
             blocks[OWN, pos, sy] = wide[pl.ds(start, MB, stride=STRIDE), :].astype(jnp.bfloat16)
 
     arrange(0)
@@ -173,15 +177,15 @@
     sib = send(SIB, 0, blocks.at[OWN], blocks.at[SIB], at_sib)
     sib_cross = [block_send(CROSS, SIB2, p, at_sib) for p in every]
     sib_relay = [block_send(RELAY, SIB2, p, at_sib) for p in every]
-    halo_up = send(HALO_LO, 0, edge.at[0], halo.at[0], at_up)
-    halo_down = send(HALO_HI, 0, edge.at[1], halo.at[1], at_down)
+    halo_up = send(HALO_HI, 0, edge.at[0], halo.at[1], at_up)
+    halo_down = send(HALO_LO, 0, edge.at[1], halo.at[0], at_down)
 
     cross[0].start()
     across[0].start()
+    cross[1].start()
+    across[1].start()
     arrange(2)
     back[0].start()
-    cross[1].start()
-    across[1].start()
     arrange(3)
     back[1].start()
     cross[2].start()
@@ -241,7 +245,7 @@
                 columns = slice(128 * k, 128 * (k + 1))
                 term_d = result[0:MB, columns]
                 yy = lax.rem(sy, 4) + k
-                row = plane * 4 + yy
+                row = plane_of(plane) * 4 + yy
                 term_r = fields[pl.ds(row, 1), :] * result[MB : 2 * MB, columns]
                 for t in range(1, K):
                     term_r = term_r + fields[pl.ds(16 * t + row, 1), :] * result[
@@ -291,7 +295,15 @@
                 part = part + diff[1 + other, sy]
             react[plane, sy] -= diffusivity_ref[sy // 4] * part
 
-    def finish():
+    def finish(pair):
+        for flipped in (0, 1):
+            planes = (2 * pair + 1, 2 * pair) if flipped else (2 * pair, 2 * pair + 1)
+
+            @pl.when(flip == flipped)
+            def _(planes=planes, block=1 - pair if flipped else pair):
+                finish_block(planes, block)
+
+    def finish_block(planes, block):
         @pl.loop(0, MB // 16, unroll=4)
         def _(n):
             rows = pl.ds(pl.multiple_of(16 * n, 16), 16)
@@ -307,24 +319,21 @@
                 return lap - 6.0 * center
 
             for s in range(2):
-                for pair in range(2):
-                    lines = []
-                    for plane in (2 * pair, 2 * pair + 1):
-                        for sy in range(4 * s, 4 * s + 4):
-                            if plane == 0:
-                                part = at(1, sy) + halo[0, sy, rows, :].astype(jnp.float32)
-                            elif plane == 1:
-                                part = at(2, sy)
-                            elif plane == 2:
-                                part = in_plane_rows(2, sy) + (at(1, sy) + at(3, sy))
-                            else:
-                                part = at(2, sy) + halo[1, sy, rows, :].astype(jnp.float32)
-                            lines.append(
-                                react[plane, sy, rows, :] - diffusivity_ref[s] * part
-                            )
-                    out_ref[rows, pl.ds(8 * (2 * s + pair), 8), :] = jnp.swapaxes(
-                        jnp.stack(lines, axis=0), 0, 1
-                    )
+                lines = []
+                for plane in planes:
+                    for sy in range(4 * s, 4 * s + 4):
+                        if plane == 0:
+                            part = at(1, sy) + halo[0, sy, rows, :].astype(jnp.float32)
+                        elif plane == 1:
+                            part = at(2, sy)
+                        elif plane == 2:
+                            part = in_plane_rows(2, sy) + (at(1, sy) + at(3, sy))
+                        else:
+                            part = at(2, sy) + halo[1, sy, rows, :].astype(jnp.float32)
+                        lines.append(react[plane, sy, rows, :] - diffusivity_ref[s] * part)
+                out_ref[rows, pl.ds(8 * (2 * s + block), 8), :] = jnp.swapaxes(
+                    jnp.stack(lines, axis=0), 0, 1
+                )
 
     take_cross(0)
     take_cross(1)
@@ -369,8 +378,9 @@
     take_relay(3)
     late(3)
     halo_down.wait_recv()
+    finish(0)
     halo_up.wait_recv()
-    finish()
+    finish(1)
 
     for copy in (*cross, *relay, *back, *across, sib, *sib_cross, halo_up, halo_down):
         copy.wait_send()

time: 29.6 us -> 29.2 us (0.986)
  the two profiles are of different devices: /device:TPU:199 before, /device:TPU:5 now
where the time goes in v5:
time: 29.2 us; the launch traced here: 28.9 us
  Pallas kernels  26.9 us (92%)
  other arithmetic  1.38 us (5%)
  between operations  0.64 us (2%)
    pallas_call x1, Pallas kernels, shards(): pl.pallas_call(kernel, name='galerkin', out_shape=(pltpu.VMEM((rows, STRI...  26.9 us
    convert_element_type x1, other arithmetic, shards(): next_field = (held - half_step * minus_rate).astype(jnp.bfloat16)  1.38 us

profile of v5, /device:TPU:5, one launch (start us, length us, event | category | flops | bytes accessed | tf_op | source)
XLA Modules:
  0.0 28.9 jit_solution(8034210568878708004)
XLA Ops:
  0.6 26.9 %galerkin.1 = (f32[64,32,128]{2,1,0:T(8,128)S(1)}, f32[64,32,128]{2,1,0:T(8,128)S(1)}) custom-call(bf16[2048,128]{1,0:T(8,128)(2,1)} %bitcast.10, bf16[5,5,64,64]{3,2,1,0:T(8,128)(2,1)} %bitcast.12, bf16[64,128]{1,0:T(8,128)(2,1)} %bitcast.13, s32[1,5]{1,0:T(1,128)} %list_hbm.1, f32[2]{0:T(128)} %diffusivity_hbm.1, f32[2,2]{1,0:T(2,128)} %mix_hbm.1, ...), custom_call_target="tpu_custom_call" | custom-call | flops 1006632960 | bytes 2097152 | tf_op jit(solution)/shard_map/galerkin/pallas_call | solution.py:404
  27.6 1.4 %subtract_convert_fusion = (bf16[64,32,128]{2,1,0:T(8,128)(2,1)}, f32[64,32,128]{2,1,0:T(8,128)}) fusion(f32[64,32,128]{2,1,0:T(8,128)S(1)} %get-tuple-element.5, f32[64,32,128]{2,1,0:T(8,128)S(1)} %get-tuple-element.4), kind=kLoop, calls=%fused_computation | loop fusion | flops 1048576 | bytes 3670016 | tf_op jit(solution)/shard_map/convert_element_type | solution.py:457

commit v6 on v5

--- a/solution.py
+++ b/solution.py
@@ -177,7 +177,10 @@
     sib = send(SIB, 0, blocks.at[OWN], blocks.at[SIB], at_sib)
     sib_cross = [block_send(CROSS, SIB2, p, at_sib) for p in every]
     sib_relay = [block_send(RELAY, SIB2, p, at_sib) for p in every]
-    halo_up = send(HALO_HI, 0, edge.at[0], halo.at[1], at_up)
+    halo_up = [
+        send(HALO_HI, s, edge.at[0, pl.ds(4 * s, 4)], halo.at[1, pl.ds(4 * s, 4)], at_up)
+        for s in (0, 1)
+    ]
     halo_down = send(HALO_LO, 0, edge.at[1], halo.at[0], at_down)
 
     cross[0].start()
@@ -226,11 +229,11 @@
         rows = pl.ds(n * 8, 8)
         held_ref[rows] = base[rows].astype(jnp.float32) + half_step * held_ref[rows]
 
-    def multiply(pos, first, last):
+    def multiply(pos, first, last, start=0, stop=4):
         plane = PLANES[pos]
         fresh = first == OWN
 
-        @pl.loop(0, 4, unroll=4)
+        @pl.loop(start, stop, unroll=stop - start)
         def _(n):
             sy = n * 2
             s = n // 2
@@ -330,7 +333,7 @@
                             part = in_plane_rows(2, sy) + (at(1, sy) + at(3, sy))
                         else:
                             part = at(2, sy) + halo[1, sy, rows, :].astype(jnp.float32)
-                        lines.append(react[plane, sy, rows, :] - diffusivity_ref[s] * part)
+                        lines.append(diffusivity_ref[s] * part - react[plane, sy, rows, :])
                 out_ref[rows, pl.ds(8 * (2 * s + block), 8), :] = jnp.swapaxes(
                     jnp.stack(lines, axis=0), 0, 1
                 )
@@ -350,13 +353,16 @@
         for dy in (1, 2, 3):
             signal(slabs_sem, device(dy, h, c))
 
-    late(0)
+    sib_cross[0].wait_recv()
+    multiply(0, RELAY, SIB2 + 1, 0, 2)
 
     @pl.when(jnp.logical_not(first))
     def _():
         pl.semaphore_wait(slabs_sem, 1)
 
-    halo_up.start()
+    halo_up[0].start()
+    multiply(0, RELAY, SIB2 + 1, 2, 4)
+    halo_up[1].start()
     take_cross(2)
     across[1].wait_recv()
     multiply(1, OWN, RELAY)
@@ -379,11 +385,27 @@
     late(3)
     halo_down.wait_recv()
     finish(0)
-    halo_up.wait_recv()
+    for copy in halo_up:
+        copy.wait_recv()
     finish(1)
 
-    for copy in (*cross, *relay, *back, *across, sib, *sib_cross, halo_up, halo_down):
+    for copy in (*cross, *relay, *back, *across, sib, *sib_cross, *halo_up, halo_down):
         copy.wait_send()
+
+
+def last_kernel(rate_ref, held_ref, rate_hbm, next_hbm, after, rate_sem, next_sem):
+    leave = pltpu.make_async_copy(rate_ref, rate_hbm, rate_sem)
+    leave.start()
+    size = MB // 2
+    copies = []
+    for n in range(2):
+        rows = pl.ds(n * size, size)
+        after[rows] = (held_ref[rows] + half_step * rate_ref[rows]).astype(jnp.bfloat16)
+        copies.append(pltpu.make_async_copy(after.at[rows], next_hbm.at[rows], next_sem.at[n]))
+        copies[-1].start()
+    for copy in copies:
+        copy.wait()
+    leave.wait()
 
 
 def shards(
@@ -401,7 +423,7 @@
     lines = species * depth
     in_hbm = pl.BlockSpec(memory_space=pltpu.HBM)
     in_vmem = pl.BlockSpec(memory_space=pltpu.VMEM)
-    minus_rate, held = pl.pallas_call(
+    rate, held = pl.pallas_call(
         kernel,
         name="galerkin",
         out_shape=(
@@ -453,8 +475,22 @@
         base_field.reshape(rows, STRIDE, width),
         prev_rate.reshape(rows, STRIDE, width),
     )
-    rate = -minus_rate
-    next_field = (held - half_step * minus_rate).astype(jnp.bfloat16)
+    rate, next_field = pl.pallas_call(
+        last_kernel,
+        name="next_section",
+        out_shape=(
+            jax.ShapeDtypeStruct((rows, STRIDE, width), jnp.float32),
+            jax.ShapeDtypeStruct((rows, STRIDE, width), jnp.bfloat16),
+        ),
+        in_specs=[in_vmem] * 2,
+        out_specs=[in_hbm] * 2,
+        scratch_shapes=[
+            pltpu.VMEM((rows, STRIDE, width), jnp.bfloat16),
+            pltpu.SemaphoreType.DMA,
+            pltpu.SemaphoreType.DMA((2,)),
+        ],
+        compiler_params=pltpu.CompilerParams(vmem_limit_bytes=16 * 1024 * 1024),
+    )(rate, held)
     return (rate.reshape(section_field.shape), next_field.reshape(section_field.shape))
 
 

time: 29.2 us -> 29 us (level)
  other arithmetic: 1.38 us -> 0 us
  Pallas kernels: 26.9 us -> 28.1 us
    convert_element_type x1 -> x0, other arithmetic: 1.38 us -> none  [shards(): next_field = (held - half_step * minus_rate).astype(jnp.bfloat16)]
    pallas_call x0 -> x1, Pallas kernels: none -> 1.16 us  [shards(): pl.pallas_call(last_kernel, name='next_section', out_shape=(jax.ShapeDtyp...]
where the time goes in v6:
time: 29 us; the launch traced here: 28.7 us
  Pallas kernels  28.1 us (97%)
  between operations  0.64 us (2%)
    pallas_call x1, Pallas kernels, shards(): pl.pallas_call(kernel, name='galerkin', out_shape=(pltpu.VMEM((rows, STRI...  26.9 us
    pallas_call x1, Pallas kernels, shards(): pl.pallas_call(last_kernel, name='next_section', out_shape=(jax.ShapeDtyp...  1.16 us

profile of v6, /device:TPU:5, one launch (start us, length us, event | category | flops | bytes accessed | tf_op | source)
XLA Modules:
  0.0 28.7 jit_solution(1349620533380530272)
XLA Ops:
  0.6 26.9 %galerkin.1 = (f32[64,32,128]{2,1,0:T(8,128)S(1)}, f32[64,32,128]{2,1,0:T(8,128)S(1)}) custom-call(bf16[2048,128]{1,0:T(8,128)(2,1)} %bitcast.9, bf16[5,5,64,64]{3,2,1,0:T(8,128)(2,1)} %bitcast.12, bf16[64,128]{1,0:T(8,128)(2,1)} %bitcast.13, s32[1,5]{1,0:T(1,128)} %list_hbm.1, f32[2]{0:T(128)} %diffusivity_hbm.1, f32[2,2]{1,0:T(2,128)} %mix_hbm.1, ...), custom_call_target="tpu_custom_call" | custom-call | flops 1006632960 | bytes 2097152 | tf_op jit(solution)/shard_map/galerkin/pallas_call | solution.py:426
  27.6 1.2 %next_section.1 = (f32[64,32,128]{2,1,0:T(8,128)}, bf16[64,32,128]{2,1,0:T(8,128)(2,1)}) custom-call(f32[64,32,128]{2,1,0:T(8,128)S(1)} %get-tuple-element.6.rate_ref, f32[64,32,128]{2,1,0:T(8,128)S(1)} %get-tuple-element.7.held_ref), custom_call_target="tpu_custom_call" | custom-call | tf_op jit(solution)/shard_map/next_section/pallas_call | solution.py:478

commit v7 on v6

--- a/solution.py
+++ b/solution.py
@@ -177,10 +177,7 @@
     sib = send(SIB, 0, blocks.at[OWN], blocks.at[SIB], at_sib)
     sib_cross = [block_send(CROSS, SIB2, p, at_sib) for p in every]
     sib_relay = [block_send(RELAY, SIB2, p, at_sib) for p in every]
-    halo_up = [
-        send(HALO_HI, s, edge.at[0, pl.ds(4 * s, 4)], halo.at[1, pl.ds(4 * s, 4)], at_up)
-        for s in (0, 1)
-    ]
+    halo_up = send(HALO_HI, 0, edge.at[0], halo.at[1], at_up)
     halo_down = send(HALO_LO, 0, edge.at[1], halo.at[0], at_down)
 
     cross[0].start()
@@ -229,11 +226,11 @@
         rows = pl.ds(n * 8, 8)
         held_ref[rows] = base[rows].astype(jnp.float32) + half_step * held_ref[rows]
 
-    def multiply(pos, first, last, start=0, stop=4):
+    def multiply(pos, first, last):
         plane = PLANES[pos]
         fresh = first == OWN
 
-        @pl.loop(start, stop, unroll=stop - start)
+        @pl.loop(0, 4, unroll=4)
         def _(n):
             sy = n * 2
             s = n // 2
@@ -353,16 +350,13 @@
         for dy in (1, 2, 3):
             signal(slabs_sem, device(dy, h, c))
 
-    sib_cross[0].wait_recv()
-    multiply(0, RELAY, SIB2 + 1, 0, 2)
+    late(0)
 
     @pl.when(jnp.logical_not(first))
     def _():
         pl.semaphore_wait(slabs_sem, 1)
 
-    halo_up[0].start()
-    multiply(0, RELAY, SIB2 + 1, 2, 4)
-    halo_up[1].start()
+    halo_up.start()
     take_cross(2)
     across[1].wait_recv()
     multiply(1, OWN, RELAY)
@@ -385,11 +379,10 @@
     late(3)
     halo_down.wait_recv()
     finish(0)
-    for copy in halo_up:
-        copy.wait_recv()
+    halo_up.wait_recv()
     finish(1)
 
-    for copy in (*cross, *relay, *back, *across, sib, *sib_cross, *halo_up, halo_down):
+    for copy in (*cross, *relay, *back, *across, sib, *sib_cross, halo_up, halo_down):
         copy.wait_send()
 
 

time: 29 us -> 29 us (level)
  no operation moved by 1% of the time
where the time goes in v7:
time: 29 us; the launch traced here: 28.7 us
  Pallas kernels  28.1 us (97%)
  between operations  0.64 us (2%)
    pallas_call x1, Pallas kernels, shards(): pl.pallas_call(kernel, name='galerkin', out_shape=(pltpu.VMEM((rows, STRI...  26.9 us
    pallas_call x1, Pallas kernels, shards(): pl.pallas_call(last_kernel, name='next_section', out_shape=(jax.ShapeDtyp...  1.16 us

profile of v7, /device:TPU:5, one launch (start us, length us, event | category | flops | bytes accessed | tf_op | source)
XLA Modules:
  0.0 28.7 jit_solution(14393848748408429288)
XLA Ops:
  0.6 26.9 %galerkin.1 = (f32[64,32,128]{2,1,0:T(8,128)S(1)}, f32[64,32,128]{2,1,0:T(8,128)S(1)}) custom-call(bf16[2048,128]{1,0:T(8,128)(2,1)} %bitcast.9, bf16[5,5,64,64]{3,2,1,0:T(8,128)(2,1)} %bitcast.12, bf16[64,128]{1,0:T(8,128)(2,1)} %bitcast.13, s32[1,5]{1,0:T(1,128)} %list_hbm.1, f32[2]{0:T(128)} %diffusivity_hbm.1, f32[2,2]{1,0:T(2,128)} %mix_hbm.1, ...), custom_call_target="tpu_custom_call" | custom-call | flops 1006632960 | bytes 2097152 | tf_op jit(solution)/shard_map/galerkin/pallas_call | solution.py:419
  27.6 1.2 %next_section.1 = (f32[64,32,128]{2,1,0:T(8,128)}, bf16[64,32,128]{2,1,0:T(8,128)(2,1)}) custom-call(f32[64,32,128]{2,1,0:T(8,128)S(1)} %get-tuple-element.6.rate_ref, f32[64,32,128]{2,1,0:T(8,128)S(1)} %get-tuple-element.7.held_ref), custom_call_target="tpu_custom_call" | custom-call | tf_op jit(solution)/shard_map/next_section/pallas_call | solution.py:471

commit v8 on v7

--- a/solution.py
+++ b/solution.py
@@ -351,13 +351,13 @@
             signal(slabs_sem, device(dy, h, c))
 
     late(0)
+    take_cross(2)
 
     @pl.when(jnp.logical_not(first))
     def _():
         pl.semaphore_wait(slabs_sem, 1)
 
     halo_up.start()
-    take_cross(2)
     across[1].wait_recv()
     multiply(1, OWN, RELAY)
     back[1].wait_recv()

time: 29 us -> 29.3 us (1.010)
  Pallas kernels: 28.1 us -> 28.6 us
    pallas_call x1, Pallas kernels: 26.9 us -> 27.4 us  [shards(): pl.pallas_call(kernel, name='galerkin', out_shape=(pltpu.VMEM((rows, STRI...]
where the time goes in v8:
time: 29.3 us; the launch traced here: 29.2 us
  Pallas kernels  28.6 us (98%)
  between operations  0.64 us (2%)
    pallas_call x1, Pallas kernels, shards(): pl.pallas_call(kernel, name='galerkin', out_shape=(pltpu.VMEM((rows, STRI...  27.4 us
    pallas_call x1, Pallas kernels, shards(): pl.pallas_call(last_kernel, name='next_section', out_shape=(jax.ShapeDtyp...  1.16 us

profile of v8, /device:TPU:5, one launch (start us, length us, event | category | flops | bytes accessed | tf_op | source)
XLA Modules:
  0.0 29.2 jit_solution(8688569149810137765)
XLA Ops:
  0.6 27.4 %galerkin.1 = (f32[64,32,128]{2,1,0:T(8,128)S(1)}, f32[64,32,128]{2,1,0:T(8,128)S(1)}) custom-call(bf16[2048,128]{1,0:T(8,128)(2,1)} %bitcast.9, bf16[5,5,64,64]{3,2,1,0:T(8,128)(2,1)} %bitcast.12, bf16[64,128]{1,0:T(8,128)(2,1)} %bitcast.13, s32[1,5]{1,0:T(1,128)} %list_hbm.1, f32[2]{0:T(128)} %diffusivity_hbm.1, f32[2,2]{1,0:T(2,128)} %mix_hbm.1, ...), custom_call_target="tpu_custom_call" | custom-call | flops 1006632960 | bytes 2097152 | tf_op jit(solution)/shard_map/galerkin/pallas_call | solution.py:419
  28.0 1.2 %next_section.1 = (f32[64,32,128]{2,1,0:T(8,128)}, bf16[64,32,128]{2,1,0:T(8,128)(2,1)}) custom-call(f32[64,32,128]{2,1,0:T(8,128)S(1)} %get-tuple-element.6.rate_ref, f32[64,32,128]{2,1,0:T(8,128)S(1)} %get-tuple-element.7.held_ref), custom_call_target="tpu_custom_call" | custom-call | tf_op jit(solution)/shard_map/next_section/pallas_call | solution.py:471

commit v9 on v7

--- a/solution.py
+++ b/solution.py
@@ -17,7 +17,7 @@
 OWN, SIB, ACROSS, CROSS, RELAY, SIB2 = range(6)
 TRANSIT, HALO_LO, HALO_HI = 6, 7, 8
 PLANES = (3, 0, 1, 2)
-PIECE = 512
+PIECE = 1024
 STRIDE = 32
 
 

time: 29 us -> 29 us (level)
  no operation moved by 1% of the time
where the time goes in v9:
time: 29 us; the launch traced here: 28.7 us
  Pallas kernels  28.1 us (97%)
  between operations  0.64 us (2%)
    pallas_call x1, Pallas kernels, shards(): pl.pallas_call(kernel, name='galerkin', out_shape=(pltpu.VMEM((rows, STRI...  26.9 us
    pallas_call x1, Pallas kernels, shards(): pl.pallas_call(last_kernel, name='next_section', out_shape=(jax.ShapeDtyp...  1.16 us

profile of v9, /device:TPU:5, one launch (start us, length us, event | category | flops | bytes accessed | tf_op | source)
XLA Modules:
  0.0 28.7 jit_solution(3728993273057950919)
XLA Ops:
  0.6 26.9 %galerkin.1 = (f32[64,32,128]{2,1,0:T(8,128)S(1)}, f32[64,32,128]{2,1,0:T(8,128)S(1)}) custom-call(bf16[2048,128]{1,0:T(8,128)(2,1)} %bitcast.9, bf16[5,5,64,64]{3,2,1,0:T(8,128)(2,1)} %bitcast.12, bf16[64,128]{1,0:T(8,128)(2,1)} %bitcast.13, s32[1,5]{1,0:T(1,128)} %list_hbm.1, f32[2]{0:T(128)} %diffusivity_hbm.1, f32[2,2]{1,0:T(2,128)} %mix_hbm.1, ...), custom_call_target="tpu_custom_call" | custom-call | flops 1006632960 | bytes 2097152 | tf_op jit(solution)/shard_map/galerkin/pallas_call | solution.py:419
  27.5 1.2 %next_section.1 = (f32[64,32,128]{2,1,0:T(8,128)}, bf16[64,32,128]{2,1,0:T(8,128)(2,1)}) custom-call(f32[64,32,128]{2,1,0:T(8,128)S(1)} %get-tuple-element.6.rate_ref, f32[64,32,128]{2,1,0:T(8,128)S(1)} %get-tuple-element.7.held_ref), custom_call_target="tpu_custom_call" | custom-call | tf_op jit(solution)/shard_map/next_section/pallas_call | solution.py:471
